TPU v7x, 128 devices: a whole 4x4x4 slice. The times are simulated.
128 devices in a mesh: dp: 16 (over z_lo, x, core), tensor: 8 (over y, z_hi).
Axes of the slice: x: 4, y: 4, z: 4 (z_hi: 2, z_lo: 2; z = z_hi * 2 + z_lo), core: 2. Of those that a mesh axis runs over, the one named last changes fastest.
Arguments:
- block_input: bfloat16 [16, 1024, 1024], P('dp', 'tensor'), may hold values from -6 to 6
- segments: int32 [16, 1024], P('dp'), may hold values from 0 to 4, as said below
- first_gain: float32 [1024], replicated, may hold values from 0.5 to 1.5
- mamba_gate: bfloat16 [1024, 1536], P('dp', 'tensor'), may hold values from -0.1875 to 0.1875
- mamba_input: bfloat16 [1024, 1536], P('dp', 'tensor'), may hold values from -0.1875 to 0.1875
- step_weight: bfloat16 [1024, 24], P('dp', 'tensor'), may hold values from -0.1875 to 0.1875
- state_weight: bfloat16 [1024, 256], P(('dp', 'tensor')), may hold values from -0.1875 to 0.1875
- conv_inner: float32 [4, 1536], P(None, 'tensor'), may hold values from -2.5 to 2.5
- conv_state: float32 [4, 256], replicated, may hold values from -2.5 to 2.5
- decay_log: float32 [24], P('tensor'), may hold values from -5.3 to 1.1
- step_bias: float32 [24], P('tensor'), may hold values from -5 to -3
- skip_scale: float32 [24], P('tensor'), may hold values from 0.5 to 1.5
- query_weight: bfloat16 [1024, 512], P('dp', 'tensor'), may hold values from -0.1875 to 0.1875
- keyval_weight: bfloat16 [1024, 256], P(('dp', 'tensor')), may hold values from -0.1875 to 0.1875
- mamba_out: bfloat16 [1536, 1024], P('tensor', 'dp'), may hold values from -0.15625 to 0.15625
- attention_out: bfloat16 [512, 1024], P('tensor', 'dp'), may hold values from -2 to 2
- second_gain: float32 [1024], replicated, may hold values from 0.5 to 1.5
- feed_gate: bfloat16 [1024, 2048], P('dp', 'tensor'), may hold values from -0.1875 to 0.1875
- feed_up: bfloat16 [1024, 2048], P('dp', 'tensor'), may hold values from -0.1875 to 0.1875
- feed_down: bfloat16 [2048, 1024], P('tensor', 'dp'), may hold values from -0.125 to 0.125
- cotangent: bfloat16 [16, 1024, 1024], P('dp', 'tensor'), may hold values from -6 to 6
Outputs:
- block_output: bfloat16 [16, 1024, 1024], P('dp', 'tensor')
- input_grad: float32 [16, 1024, 1024], P('dp', 'tensor')
- first_gain_grad: float32 [1024], replicated
- mamba_gate_grad: float32 [1024, 1536], P('dp', 'tensor')
- mamba_input_grad: float32 [1024, 1536], P('dp', 'tensor')
- step_weight_grad: float32 [1024, 24], P('dp', 'tensor')
- state_weight_grad: float32 [1024, 256], P(('dp', 'tensor'))
- conv_inner_grad: float32 [4, 1536], P(None, 'tensor')
- conv_state_grad: float32 [4, 256], replicated
- decay_log_grad: float32 [24], P('tensor')
- step_bias_grad: float32 [24], P('tensor')
- skip_scale_grad: float32 [24], P('tensor')
- query_weight_grad: float32 [1024, 512], P('dp', 'tensor')
- keyval_weight_grad: float32 [1024, 256], P(('dp', 'tensor'))
- mamba_out_grad: float32 [1536, 1024], P('tensor', 'dp')
- attention_out_grad: float32 [512, 1024], P('tensor', 'dp')
- second_gain_grad: float32 [1024], replicated
- feed_gate_grad: float32 [1024, 2048], P('dp', 'tensor')
- feed_up_grad: float32 [1024, 2048], P('dp', 'tensor')
- feed_down_grad: float32 [2048, 1024], P('tensor', 'dp')
Inputs may be any that keep to these rules, and one draw needn't show every extreme that they name: `segments`: in each row of 1024 positions the numbers start at 0, never fall and rise by one at four places, and segment 2 holds every position from 64 to 959.
All inputs are finite; a program needn't handle non-finite values.
Results may differ from a plain program's by a relative error of at most 0.028.
Values may be sent and summed in bfloat16 or wider, within the bound.
No kernel may reach another device: no remote copies, remote signals or barrier semaphores. Data moves between devices by JAX's collectives and lax.ppermute only.
A program may use at most 192 MiB of HBM per device.

v0:
```python
import jax
import jax.numpy as jnp
import numpy as np
from jax import lax
from jax.experimental import pallas as pl
from jax.experimental.pallas import tpu as pltpu
from jax.sharding import PartitionSpec as P

QHEADS = 8
KVHEADS = 2
AHDIM = 64
TOKENS = 1024
WIDTH = 1024
BLOCK = 128
BLOCKS = TOKENS // BLOCK
HEADS = 3
HDIM = 64
INNER = HEADS * HDIM
FEED = 256
QUERY_BLOCK = 256
NORM_EPS = 1e-05
ROPE_BASE = 10000.0
MASKED = -1e30
VMEM_BYTES = 60 * 1024 * 1024

KV_AT = 0
CONV_AT = 128
GATE_AT = 640
QS_AT = 896
PACKED = 1024
EARLY = 384
SENT = 896
PAYLOAD = 32
CONV_WIDTH = 512
STEP_LANE = 64

CHIPS = ("zlo", "xh", "xl")
FEED16 = ("yh", *CHIPS)
TENSOR = ("yh", "yl", "zhi")
NEAR = ("yl", "zhi")
PIECE = BLOCK + 16
WIDE = 1152
FINE_SIZES = (2,) * 7

F32 = jnp.float32
BF16 = jnp.bfloat16


def dot(a, b):
    return lax.dot_general(a, b, (((1,), (0,)), ((), ())), preferred_element_type=F32)


def dot_right(a, b):
    return lax.dot_general(a, b, (((1,), (1,)), ((), ())), preferred_element_type=F32)


def dot_left(a, b):
    return lax.dot_general(a, b, (((0,), (0,)), ((), ())), preferred_element_type=F32)


def parts_of(values, terms):
    parts = []
    for _ in range(terms - 1):
        part = values.astype(BF16)
        parts.append(part)
        values = values - part.astype(F32)
    parts.append(values.astype(BF16))
    return parts


def times_ones(values, ones, terms=2):
    return sum(dot(part, ones) for part in parts_of(values, terms))


def ones_times(ones, values, terms=2):
    return sum(dot(ones, part) for part in parts_of(values, terms))


def iota(shape, dim):
    return lax.broadcasted_iota(jnp.int32, shape, dim)


def softplus(v):
    return jnp.maximum(v, 0.0) + jnp.log1p(jnp.exp(-jnp.abs(v)))


def sigmoid(v):
    return 1.0 / (1.0 + jnp.exp(-v))


def head_matrices():
    lane, channel = (iota((BLOCK, 256), 0), iota((BLOCK, 256), 1))
    spread = ((channel >> 6) + STEP_LANE == lane) & (channel < INNER)
    lane, channel = (iota((256, BLOCK), 1), iota((256, BLOCK), 0))
    gather = ((channel >> 6) + STEP_LANE == lane) & (channel < INNER)
    return (spread.astype(BF16), gather.astype(BF16))


def per_head(values):
    of_head = iota(values.shape, 1) >> 6
    return jnp.concatenate(
        [jnp.where(of_head == h, values, jnp.zeros_like(values)) for h in range(HEADS)], axis=0
    )


def conv_parts(proj_ref, par_ref, aux, start):
    here = proj_ref[pl.ds(start, BLOCK), CONV_AT:GATE_AT]
    before = proj_ref[pl.ds(pl.multiple_of(jnp.maximum(start - 8, 0), 8), 8), CONV_AT:GATE_AT]
    both = jnp.concatenate([before, here], axis=0)
    lagged = [here]
    for lag in range(1, 4):
        lagged.append(both[8 - lag : 8 - lag + BLOCK] * aux[:, lag : lag + 1])
    pre = sum(lagged[lag] * par_ref[lag : lag + 1, :] for lag in range(4))
    return (lagged, pre)


def step_parts(proj_ref, par_ref, aux, lower, start):
    raw = proj_ref[pl.ds(start, BLOCK), QS_AT:PACKED] + par_ref[8:9, 0:128]
    lane = iota((BLOCK, 128), 1)
    is_head = (lane >= STEP_LANE) & (lane < STEP_LANE + HEADS)
    step = jnp.where(is_head, softplus(raw), 0.0)
    rate = -step * jnp.exp(par_ref[9:10, 0:128])
    total = ones_times(lower, rate, 3)
    reach = aux[:, 4:5] * jnp.exp(total)
    to_end = aux[:, 5:6] * jnp.exp(total[BLOCK - 1 : BLOCK, :] - total)
    return (raw, is_head, step, rate, total, reach, to_end)


def decay_of(total, total_rows, keep, h):
    at = STEP_LANE + h
    gap = total[:, at : at + 1] - total_rows[at : at + 1, :]
    return jnp.exp(jnp.where(keep, gap, MASKED))


def turn_halves(values, rope, back):
    up = pltpu.roll(values, 96, 1) * rope[:, 128:256]
    down = pltpu.roll(values, 32, 1) * rope[:, 256:384]
    here = values * rope[:, 0:128]
    return here - up - down if back else here + up + down


def allowed_keys(aux_ref, segrow_ref, first, count):
    query_seg = aux_ref[first : first + QUERY_BLOCK, 0:1]
    key_seg = segrow_ref[0:1, 0:count]
    shape = (QUERY_BLOCK, count)
    return (query_seg == key_seg) & (iota(shape, 1) <= iota(shape, 0) + first)


def fold(line):
    return jnp.concatenate([line[:, 128 * i : 128 * i + 128] for i in range(8)], axis=0)


def begin(pairs, sems, first=0):
    copies = [
        pltpu.make_async_copy(source, target, sems.at[first + at])
        for at, (source, target) in enumerate(pairs)
    ]
    for copy in copies:
        copy.start()
    return copies


def finish(*copies):
    for copy in copies:
        copy.wait()


def join_cores(core, own, mate, whole, sems, first):
    lead = (slice(None),) * (len(whole.shape) - 3)
    pairs = [(own, whole.at[(*lead, core)]), (mate, whole.at[(*lead, 1 - core)])]
    return begin(pairs, sems, first)


def split_cores(core, whole, keep, send, sems, first):
    lead = (slice(None),) * (len(whole.shape) - 3)
    pairs = [(whole.at[(*lead, core)], keep), (whole.at[(*lead, 1 - core)], send)]
    return begin(pairs, sems, first)


def columns(ref, first, last):
    return ref[:, :, :, first:last].reshape(WIDTH, last - first)


def mixer_forward_kernel(
    core_ref,
    p0,
    p1,
    p2,
    p3,
    p4,
    p5,
    p6,
    p7,
    own_hbm,
    mate_hbm,
    rope_hbm,
    aux_hbm,
    segrow_ref,
    par_ref,
    normed_hbm,
    mix_hbm,
    proj_hbm,
    states_hbm,
    qkv_hbm,
    lse_hbm,
    heads_hbm,
    normed_ref,
    w_ref,
    rope_ref,
    aux_ref,
    mix_ref,
    proj_ref,
    states_ref,
    qkv_ref,
    lse_ref,
    heads_ref,
    in_sems,
    out_sems,
):
    pieces = [
        (piece, normed_ref.at[core_ref[2] ^ k])
        for k, piece in enumerate((p0, p1, p2, p3, p4, p5, p6, p7))
    ]
    first_come = begin(pieces, in_sems, 0)
    first_come += join_cores(core_ref[0], own_hbm, mate_hbm, w_ref, in_sems, 8)
    come = begin([(rope_hbm, rope_ref), (aux_hbm, aux_ref)], in_sems, 10)
    finish(*first_come)
    gone = begin([(normed_ref, normed_hbm)], out_sems, 10)
    for chunk in range(4):
        rows = slice(256 * chunk, 256 * chunk + 256)
        normed = normed_ref[2 * chunk : 2 * chunk + 2].reshape(256, WIDTH)
        state = dot(normed, columns(w_ref, 0, 512))
        proj_ref[rows, CONV_AT : CONV_AT + 256] = state[:, 0:256]
        proj_ref[rows, KV_AT:CONV_AT] = state[:, 256:384]
        proj_ref[rows, QS_AT:PACKED] = state[:, 384:512]
        inner = dot(normed, columns(w_ref, 512, SENT))
        real = iota((256, 256), 1) < INNER
        gate = jnp.concatenate([inner[:, INNER:], inner[:, 0:64]], axis=1)
        proj_ref[rows, CONV_AT + 256 : GATE_AT] = jnp.where(real, inner[:, 0:256], 0.0)
        proj_ref[rows, GATE_AT:QS_AT] = jnp.where(real, gate, 0.0)
    gone += begin([(proj_ref, proj_hbm)], out_sems, 1)
    finish(*come)
    lane = iota((256, 128), 1)
    for first in range(0, TOKENS, 256):
        rows = slice(first, first + 256)
        rope = rope_ref[rows, :]
        keyval = proj_ref[rows, KV_AT:CONV_AT]
        turned = turn_halves(proj_ref[rows, QS_AT:PACKED], rope, False)
        qkv_ref[rows, 0:128] = (turned * AHDIM**-0.5).astype(BF16)
        qkv_ref[rows, 128:256] = turn_halves(keyval, rope, False).astype(BF16)
        ones = jnp.where(lane == 0, 1.0, 0.0)
        qkv_ref[rows, 256:384] = jnp.where(lane >= 64, keyval, ones).astype(BF16)
    gone += begin([(qkv_ref, qkv_hbm)], out_sems, 2)
    for first in range(0, TOKENS, QUERY_BLOCK):
        rows = slice(first, first + QUERY_BLOCK)
        count = first + QUERY_BLOCK
        scores = dot_right(qkv_ref[rows, 0:128], qkv_ref[0:count, 128:256])
        scores = jnp.where(allowed_keys(aux_ref, segrow_ref, first, count), scores, MASKED)
        top = jnp.max(scores, axis=1, keepdims=True)
        raised = jnp.exp(scores - top)
        summed = dot(raised.astype(BF16), qkv_ref[0:count, 256:384])
        total = summed[:, 0:1]
        heads_ref[rows, 128:256] = jnp.where(lane >= 64, summed / total, 0.0).astype(BF16)
        lse_ref[rows, :] = jnp.broadcast_to(top + jnp.log(total), (QUERY_BLOCK, 128))

    gone += begin([(lse_ref, lse_hbm)], out_sems, 3)

    spread, _ = head_matrices()
    causal = iota((BLOCK, BLOCK), 0) >= iota((BLOCK, BLOCK), 1)
    lower = causal.astype(BF16)

    def block_step(index, state):
        start = pl.multiple_of(index * BLOCK, BLOCK)
        rows = pl.ds(start, BLOCK)
        aux = aux_ref[rows, :]
        _, pre = conv_parts(proj_ref, par_ref, aux, start)
        conv = (pre * sigmoid(pre)).astype(BF16)
        in_map, out_map, inner = (conv[:, 0:128], conv[:, 128:256], conv[:, 256:512].astype(F32))
        _, _, step, _, total, reach, to_end = step_parts(proj_ref, par_ref, aux, lower, start)
        wide = times_ones(jnp.concatenate([step, reach, to_end], axis=0), spread)
        step_wide, reach_wide, end_wide = (wide[0:128], wide[128:256], wide[256:384])
        stepped = inner * step_wide
        keep = causal & (aux[:, 0:1] == segrow_ref[0:1, pl.ds(start, BLOCK)])
        total_rows = jnp.transpose(total)
        shared = dot_right(out_map, in_map)
        mixing = jnp.concatenate(
            [(decay_of(total, total_rows, keep, h) * shared).astype(BF16) for h in range(HEADS)],
            axis=1,
        )
        states_ref[rows, :] = state
        result = dot(mixing, per_head(stepped).astype(BF16))
        result = result + dot(out_map, state.astype(BF16)) * reach_wide
        result = result + inner * par_ref[10:11, 0:256]
        gate = proj_ref[rows, GATE_AT:QS_AT]
        gated = (result * (gate * sigmoid(gate))).astype(BF16)
        heads_ref[rows, 0:128] = gated[:, 0:128]
        heads_ref[rows, 128:256] = heads_ref[rows, 128:256] + gated[:, 128:256]
        added = dot_left(in_map, (stepped * end_wide).astype(BF16))
        return state * reach_wide[BLOCK - 1 : BLOCK, :] + added

    lax.fori_loop(0, BLOCKS, block_step, jnp.zeros((BLOCK, 256), F32), unroll=UNROLL)
    gone += begin([(states_ref, states_hbm), (heads_ref, heads_hbm)], out_sems, 4)
    w2 = columns(w_ref, SENT, WIDE)
    for chunk in range(4):
        rows = slice(256 * chunk, 256 * chunk + 256)
        mix_ref[rows, :] = dot_right(heads_ref[rows, :], w2).astype(BF16)
        gone += begin([(mix_ref.at[rows, :], mix_hbm.at[rows, :])], out_sems, 6 + chunk)
    finish(*gone)


def mixer_backward_kernel(
    core_ref,
    mixgrad_hbm,
    own_hbm,
    mate_hbm,
    qkv_hbm,
    lse_hbm,
    aux_hbm,
    rope_hbm,
    proj_hbm,
    states_hbm,
    normed_hbm,
    segrow_ref,
    par_ref,
    second_ref,
    ngrad_hbm,
    dproj_hbm,
    small_ref,
    mixgrad_ref,
    w_ref,
    qkv_ref,
    lse_ref,
    aux_ref,
    rope_ref,
    proj_ref,
    states_ref,
    normed_ref,
    mix_ref,
    dproj_ref,
    d_ref,
    dkv_ref,
    in_sems,
    out_sems,
):
    first_come = begin([(mixgrad_hbm, mixgrad_ref)], in_sems, 0)
    first_come += join_cores(core_ref[0], own_hbm, mate_hbm, w_ref, in_sems, 1)
    come = begin(
        [
            (qkv_hbm, qkv_ref),
            (lse_hbm, lse_ref),
            (aux_hbm, aux_ref),
            (rope_hbm, rope_ref),
            (proj_hbm, proj_ref),
            (states_hbm, states_ref),
            (normed_hbm, normed_ref),
        ],
        in_sems,
        3,
    )
    finish(*first_come)
    gone = []
    w2 = columns(w_ref, SENT, WIDE)
    for first in range(0, TOKENS, 256):
        rows = slice(first, first + 256)
        d_ref[rows, :] = dot(mixgrad_ref[rows, :], w2)
    lane = iota((QUERY_BLOCK, 128), 1)
    dkv_ref[...] = jnp.zeros_like(dkv_ref)
    finish(*come[0:3])
    for first in range(0, TOKENS, QUERY_BLOCK):
        rows = slice(first, first + QUERY_BLOCK)
        count = first + QUERY_BLOCK
        queries, keys = (qkv_ref[rows, 0:128], qkv_ref[0:count, 128:256])
        out_grad = jnp.where(lane >= 64, d_ref[rows, 128:256], 0.0).astype(BF16)
        scores = dot_right(queries, keys) - lse_ref[rows, 0:1]
        weights = jnp.exp(
            jnp.where(allowed_keys(aux_ref, segrow_ref, first, count), scores, MASKED)
        )
        weight_grad = dot_right(out_grad, qkv_ref[0:count, 256:384])
        mean = jnp.sum(weights * weight_grad, axis=1, keepdims=True)
        score_grad = (weights * (weight_grad - mean)).astype(BF16)
        query_grad = dot(score_grad, keys) * AHDIM**-0.5
        d_ref[rows, 128:256] = jnp.where(
            lane < 64, d_ref[rows, 128:256], pltpu.roll(query_grad, 64, 1)
        )
        dkv_ref[0:count, 0:128] += dot_left(score_grad, queries)
        dkv_ref[0:count, 128:256] += dot_left(weights.astype(BF16), out_grad)
    finish(come[3])
    for first in range(0, TOKENS, 256):
        rows = slice(first, first + 256)
        rope = rope_ref[rows, :]
        query_grad = turn_halves(pltpu.roll(d_ref[rows, 128:256], 64, 1), rope, True)
        dproj_ref[rows, 384:512] = query_grad.astype(BF16)
        key_grad = turn_halves(dkv_ref[rows, 0:128], rope, True)
        keyval_grad = jnp.where(lane < 64, key_grad, dkv_ref[rows, 128:256])
        dproj_ref[rows, 256:384] = keyval_grad.astype(BF16)

    spread, gather = head_matrices()
    row, column = (iota((BLOCK, BLOCK), 0), iota((BLOCK, BLOCK), 1))
    causal = row >= column
    lower = causal.astype(BF16)
    upper = (row <= column).astype(BF16)
    strict = (row > column).astype(BF16)
    real = iota((BLOCK, 256), 1) < INNER
    head_lane = iota((BLOCK, 128), 1)

    def block_step(turn, carried):
        state_grad, later, taps_sum, head_sum, skip_sum = carried
        start = pl.multiple_of((BLOCKS - 1 - turn) * BLOCK, BLOCK)
        rows = pl.ds(start, BLOCK)
        aux = aux_ref[rows, :]
        lagged, pre = conv_parts(proj_ref, par_ref, aux, start)
        sig = sigmoid(pre)
        conv = (pre * sig).astype(BF16)
        in_map, out_map, inner = (conv[:, 0:128], conv[:, 128:256], conv[:, 256:512].astype(F32))
        raw, is_head, step, rate, total, reach, to_end = step_parts(
            proj_ref, par_ref, aux, lower, start
        )
        wide = times_ones(jnp.concatenate([step, reach, to_end], axis=0), spread)
        step_wide, reach_wide, end_wide = (wide[0:128], wide[128:256], wide[256:384])
        stepped = inner * step_wide
        stepped_low = stepped.astype(BF16)
        keep = causal & (aux[:, 0:1] == segrow_ref[0:1, pl.ds(start, BLOCK)])
        total_rows = jnp.transpose(total)
        shared = dot_right(out_map, in_map)
        decays = [decay_of(total, total_rows, keep, h) for h in range(HEADS)]
        mixing = [(decay * shared).astype(BF16) for decay in decays]
        state = states_ref[rows, :]
        state_low = state.astype(BF16)
        incoming = dot(out_map, state_low) * reach_wide
        result = dot(jnp.concatenate(mixing, axis=1), per_head(stepped).astype(BF16)) + incoming
        result = result + inner * par_ref[10:11, 0:256]

        gate = proj_ref[rows, GATE_AT:QS_AT]
        gate_sig = sigmoid(gate)
        gated_grad = jnp.where(real, d_ref[rows, :], 0.0)
        gate_grad = gated_grad * result * (gate_sig * (1.0 + gate * (1.0 - gate_sig)))
        out_grad = gated_grad * (gate * gate_sig)
        by_head = per_head(out_grad).astype(BF16)

        mixing_grad = dot_right(by_head, stepped_low)
        shared_grad = jnp.zeros((BLOCK, BLOCK), F32)
        edges = []
        for h in range(HEADS):
            decayed = mixing_grad[h * BLOCK : (h + 1) * BLOCK] * decays[h]
            shared_grad = shared_grad + decayed
            edges.append((decayed * shared).astype(BF16))
        crossing = dot(upper, jnp.concatenate(edges, axis=1))
        rate_grad = jnp.zeros((BLOCK, 128), F32)
        for h in range(HEADS):
            part = jnp.where(row > column, crossing[:, h * BLOCK : (h + 1) * BLOCK], 0.0)
            part = jnp.sum(part, axis=1, keepdims=True)
            rate_grad = rate_grad + jnp.where(head_lane == STEP_LANE + h, part, 0.0)

        reached = (out_grad * reach_wide).astype(BF16)
        state_grad_low = state_grad.astype(BF16)
        ended = dot(in_map, state_grad_low) * end_wide
        mapped = dot_left(jnp.concatenate(mixing, axis=0), by_head) + ended
        inner_grad = mapped * step_wide + out_grad * par_ref[10:11, 0:256]
        kept = jnp.sum(state_grad * state, axis=0, keepdims=True)
        kept = jnp.broadcast_to(kept * reach_wide[BLOCK - 1 : BLOCK, :], (8, 256))
        sums = times_ones(
            jnp.concatenate([inner * mapped, out_grad * incoming, stepped * ended, kept], axis=0),
            gather,
        )
        flows = ones_times(
            jnp.concatenate([upper, strict], axis=1), sums[128:384]
        )
        rate_grad = rate_grad + flows + sums[384:385]
        step_grad = sums[0:128] - jnp.exp(par_ref[9:10, 0:128]) * rate_grad
        step_grad = jnp.where(is_head, step_grad * sigmoid(raw), 0.0)
        dproj_ref[rows, 384:512] = dproj_ref[rows, 384:512] + step_grad.astype(BF16)
        head_sum = head_sum + jnp.concatenate(
            [
                jnp.sum(jnp.where(is_head, rate_grad * rate, 0.0), axis=0, keepdims=True),
                jnp.sum(step_grad, axis=0, keepdims=True),
                jnp.zeros((6, 128), F32),
            ],
            axis=0,
        )
        skip_sum = skip_sum + jnp.sum(inner * out_grad, axis=0, keepdims=True)

        shared_low = shared_grad.astype(BF16)
        out_map_grad = dot(shared_low, in_map) + dot_right(reached, state_low)
        in_map_grad = dot_left(shared_low, out_map) + dot_right(
            (stepped * end_wide).astype(BF16), state_grad_low
        )
        conv_grad = jnp.concatenate([in_map_grad, out_map_grad, inner_grad], axis=1)
        pre_grad = conv_grad * (sig * (1.0 + pre * (1.0 - sig)))
        taps_sum = taps_sum + jnp.concatenate(
            [jnp.sum(pre_grad * lagged[lag], axis=0, keepdims=True) for lag in range(4)]
            + [jnp.zeros((4, CONV_WIDTH), F32)],
            axis=0,
        )
        both = jnp.concatenate([pre_grad, later], axis=0)
        masks = aux_ref[pl.ds(start, BLOCK + 8), :]
        u_grad = pre_grad * par_ref[0:1, :]
        for lag in range(1, 4):
            shifted = (both * masks[:, lag : lag + 1])[lag : lag + BLOCK]
            u_grad = u_grad + shifted * par_ref[lag : lag + 1, :]
        dproj_ref[rows, 0:256] = u_grad[:, 0:256].astype(BF16)
        inner = jnp.concatenate([u_grad[:, 256 : 256 + INNER], gate_grad[:, 0:INNER]], axis=1)
        dproj_ref[rows, 512:SENT] = inner.astype(BF16)
        state_grad = state_grad * reach_wide[BLOCK - 1 : BLOCK, :] + dot_left(out_map, reached)
        return (state_grad, pre_grad[0:8], taps_sum, head_sum, skip_sum)

    carried = (
        jnp.zeros((BLOCK, 256), F32),
        jnp.zeros((8, CONV_WIDTH), F32),
        jnp.zeros((8, CONV_WIDTH), F32),
        jnp.zeros((8, 128), F32),
        jnp.zeros((1, 256), F32),
    )
    finish(*come[4:6])
    _, _, taps_sum, head_sum, skip_sum = lax.fori_loop(
        0, BLOCKS, block_step, carried, unroll=UNROLL
    )
    gone += begin([(dproj_ref, dproj_hbm)], out_sems, 0)
    finish(come[6])
    gain = jnp.zeros((1, WIDTH), F32)
    w1 = columns(w_ref, 0, SENT)
    for chunk in range(4):
        rows = slice(256 * chunk, 256 * chunk + 256)
        grad = dot_right(dproj_ref[rows, :], w1)
        mix_ref[rows, :] = grad.astype(BF16)
        gone += begin([(mix_ref.at[rows, :], ngrad_hbm.at[rows, :])], out_sems, 1 + chunk)
        normed = normed_ref[2 * chunk : 2 * chunk + 2].reshape(256, WIDTH)
        gain = gain + jnp.sum(grad * normed.astype(F32), axis=0, keepdims=True)
    upper_rows = jnp.concatenate([taps_sum[0:4, 0:256], taps_sum[0:4, 256:512]], axis=0)
    upper_rows = jnp.concatenate([upper_rows, fold(gain)], axis=1)
    skip_rows = jnp.concatenate([skip_sum, jnp.zeros((7, 256), F32)], axis=0)
    lower_rows = jnp.concatenate([fold(second_ref[0:1, :]), head_sum[:, 64:128], skip_rows[:, 0:INNER]], axis=1)
    small = jnp.concatenate([upper_rows, lower_rows], axis=0)
    small_ref[...] = small
    finish(*gone)


def feed_kernel(
    core_ref, n0, n1, n2, n3, c0, c1, c2, c3, own_hbm, mate_hbm,
    o0, o1, o2, o3, g0, g1, g2, g3, act_ref, grads_ref, gain_ref, w_ref, sems,
):
    finish(*join_cores(core_ref[0], own_hbm, mate_hbm, w_ref, sems, 0))
    inputs = ((n0, n1, c0, c1), (n2, n3, c2, c3))
    outs = (((o0, g0), (o1, g1)), ((o2, g2), (o3, g3)))
    gain = jnp.zeros((1, WIDTH), F32)
    for j in range(2):
        rows = slice(256 * j, 256 * j + 256)
        normed = jnp.concatenate([inputs[j][0][...], inputs[j][1][...]], axis=0)
        cot = jnp.concatenate([inputs[j][2][...], inputs[j][3][...]], axis=0)
        out_sum, grad_sum = (0.0, 0.0)
        for h in range(2):
            up_weights = columns(w_ref.at[h], 0, 512)
            down = columns(w_ref.at[h], 512, 768)
            both = dot(normed, up_weights)
            gate, up = (both[:, 0:FEED], both[:, FEED:])
            sig = sigmoid(gate)
            silu = gate * sig
            act = (silu * up).astype(BF16)
            act_ref[rows, h * FEED : (h + 1) * FEED] = act
            out_sum = out_sum + dot_right(act, down)
            act_grad = dot(cot, down)
            gate_grad = (act_grad * up * (sig + silu * (1.0 - sig))).astype(BF16)
            up_grad = (act_grad * silu).astype(BF16)
            grads = jnp.concatenate([gate_grad, up_grad], axis=1)
            grads_ref[rows, h * 512 : (h + 1) * 512] = grads
            grad_sum = grad_sum + dot_right(grads, up_weights)
        gain = gain + jnp.sum(grad_sum * normed.astype(F32), axis=0, keepdims=True)
        out_low, grad_low = (out_sum.astype(BF16), grad_sum.astype(BF16))
        for half in range(2):
            part = slice(half * BLOCK, (half + 1) * BLOCK)
            outs[j][half][0][...] = out_low[part]
            outs[j][half][1][...] = grad_low[part]
    gain_ref[...] = jnp.broadcast_to(gain, (8, WIDTH))


def feed_weights_kernel(
    core_ref, n0, n1, n2, n3, c0, c1, c2, c3, act_ref, grads_ref, keep_hbm, send_hbm, out_ref, sems
):
    normed = jnp.concatenate([r[...] for r in (n0, n1, n2, n3)], axis=0)
    cot = jnp.concatenate([r[...] for r in (c0, c1, c2, c3)], axis=0)
    up = dot_left(normed, grads_ref[...]).astype(BF16)
    down = dot_left(cot, act_ref[...]).astype(BF16)
    for h in range(2):
        up_here = up[:, h * 512 : (h + 1) * 512].reshape(8, 2, 64, 512)
        down_here = down[:, h * FEED : (h + 1) * FEED].reshape(8, 2, 64, FEED)
        out_ref[h, :, :, :, 0:512] = up_here
        out_ref[h, :, :, :, 512:768] = down_here
    finish(*split_cores(core_ref[0], out_ref, keep_hbm, send_hbm, sems, 0))


def mixer_weights_kernel(
    core_ref, normed_ref, dproj_ref, mixgrad_ref, heads_ref, keep_hbm, send_hbm, out_ref, sems
):
    normed = normed_ref[...].reshape(TOKENS, WIDTH)
    for first, last in ((0, 512), (512, SENT)):
        grad = dot_left(normed, dproj_ref[:, first:last]).astype(BF16)
        out_ref[:, :, :, first:last] = grad.reshape(8, 2, 64, last - first)
    grad = dot_left(mixgrad_ref[...], heads_ref[...]).astype(BF16)
    out_ref[:, :, :, SENT:WIDE] = grad.reshape(8, 2, 64, WIDE - SENT)
    finish(*split_cores(core_ref[0], out_ref, keep_hbm, send_hbm, sems, 0))


def mixer_pair_kernel(keep_ref, come_ref, small_ref, small_come_ref, out_ref):
    total = keep_ref[...].astype(F32) + come_ref[...].astype(F32)
    small = small_ref[...] + small_come_ref[...]
    high = small.astype(BF16)
    low = (small - high.astype(F32)).astype(BF16)
    tail = jnp.concatenate([high, low, jnp.zeros_like(high)], axis=1)
    for i in range(8):
        out_ref[i, 0:64, :] = total[i].astype(BF16)
        out_ref[i, 64:, :] = tail


def feed_pair_kernel(keep_ref, come_ref, out_ref):
    out_ref[...] = (keep_ref[...].astype(F32) + come_ref[...].astype(F32)).astype(BF16)


def collect_kernel(
    core_ref, blocks_ref, lines_ref, gate_ref, input_ref, step_ref, query_ref, mamba_ref, attend_ref,
    own_ref,
):
    total = total_rows(blocks_ref)
    own = total[64:, 0:EARLY] + total[64:, EARLY : 2 * EARLY]
    total = total[0:64]
    keyval = total[:, 256:384]
    turned = pltpu.roll(keyval, AHDIM, 1)
    low = iota(keyval.shape, 1) < AHDIM
    first = core_ref[1] == 0
    keys = jnp.where(first, jnp.where(low, keyval, 0.0), jnp.where(low, 0.0, turned))
    values = jnp.where(first, jnp.where(low, turned, 0.0), jnp.where(low, 0.0, keyval))
    shared = jnp.concatenate([total[:, 0:256], keys, values], axis=1)
    for t in range(8):
        lines_ref[t, 0:8, :] = shared[8 * t : 8 * t + 8]
        lines_ref[t, 8:24, 0:EARLY] = own
        lines_ref[t, 8:24, EARLY:] = jnp.zeros((16, 512 - EARLY), F32)
    own_ref[...] = own
    query_ref[...] = total[:, EARLY : EARLY + AHDIM]
    step_ref[...] = total[:, EARLY + STEP_LANE : EARLY + STEP_LANE + HEADS]
    input_ref[...] = total[:, 512 : 512 + INNER]
    gate_ref[...] = total[:, 512 + INNER : SENT]
    turned = jnp.transpose(total[:, SENT:WIDE])
    mamba_ref[...] = turned[0:INNER]
    attend_ref[...] = turned[INNER:]


def last_kernel(
    lines_ref, gain_one_ref, gain_two_ref, state_ref, keyval_ref, taps_ref, first_ref, second_ref
):
    pairs = [lines_ref[2 * t] + lines_ref[2 * t + 1] for t in range(4)]
    total = (pairs[0] + pairs[1]) + (pairs[2] + pairs[3])
    state_ref[...] = total[0:8, 0:256]
    keyval_ref[...] = total[0:8, 256:512]
    taps_ref[...] = total[8:12, 0:256]
    first_ref[...] = total[8:16, 256:384] / gain_one_ref[...]
    second_ref[...] = total[16:24, 0:128] / gain_two_ref[...]


def total_of(pieces):
    return sum(piece[...].astype(F32) for piece in pieces)


def total_rows(blocks_ref):
    return sum(blocks_ref[i].astype(F32) for i in range(8))


def row_norm(values):
    return lax.rsqrt(jnp.mean(values * values, axis=-1, keepdims=True) + NORM_EPS)


def norm_back(values, gain, grad):
    scale = row_norm(values)
    scaled = grad * gain
    return scale * scaled - values * (
        scale**3 * jnp.mean(scaled * values, axis=-1, keepdims=True)
    )


def first_norm_kernel(x_ref, gain_ref, normed_ref):
    x = x_ref[...].astype(F32)
    normed_ref[...] = (x * row_norm(x) * gain_ref[...]).astype(BF16)


def second_norm_kernel(x_ref, gain_ref, blocks_ref, hidden_ref, normed_ref):
    hidden = x_ref[...].astype(F32) + total_rows(blocks_ref)
    hidden_ref[...] = hidden
    normed_ref[...] = (hidden * row_norm(hidden) * gain_ref[...]).astype(BF16)


def hidden_grad_kernel(hidden_ref, gain_ref, cot_ref, s0, s1, s2, s3, grad_ref, low_ref):
    back = norm_back(hidden_ref[...], gain_ref[...], total_of((s0, s1, s2, s3)))
    grad = cot_ref[...].astype(F32) + back
    grad_ref[...] = grad
    low = grad.astype(BF16)
    for i in range(8):
        low_ref[i] = low


def input_grad_kernel(x_ref, gain_ref, hidden_grad_ref, blocks_ref, grad_ref):
    x = x_ref[...].astype(F32)
    back = norm_back(x, gain_ref[...], total_rows(blocks_ref))
    grad_ref[...] = hidden_grad_ref[...] + back


def output_kernel(hidden_ref, s0, s1, s2, s3, out_ref):
    out_ref[...] = (hidden_ref[...] + total_of((s0, s1, s2, s3))).astype(BF16)


def like(dtype, *shape):
    return jax.ShapeDtypeStruct(shape, dtype)


VMEM = pl.BlockSpec(memory_space=pltpu.VMEM)
SMEM = pl.BlockSpec(memory_space=pltpu.SMEM)
ANY = pl.BlockSpec(memory_space=pl.ANY)


def run(kernel, name, outs, args, specs=None, scratch=(), us=0.05, out_specs=None):
    return pl.pallas_call(
        kernel,
        in_specs=specs or [VMEM] * len(args),
        out_specs=out_specs or [VMEM] * len(outs),
        out_shape=list(outs),
        scratch_shapes=list(scratch),
        compiler_params=pltpu.CompilerParams(vmem_limit_bytes=VMEM_BYTES),
        cost_estimate=pl.CostEstimate(
            flops=int(us * 1e9), transcendentals=0, bytes_accessed=int(us * 2e6)
        ),
        name=name,
    )(*args)


def held(array):
    return pltpu.VMEM(array.shape, array.dtype)


HERE = (BLOCK, WIDTH)
UNROLL = 2
FORWARD_US = 20
BACKWARD_US = 33
ROW = (8, BLOCK, WIDTH)


def mixer_forward(core, pieces, own, mate, aux, segrow, pack, rope):
    outs = (
        like(BF16, *ROW),
        like(BF16, TOKENS, WIDTH),
        like(F32, TOKENS, PACKED),
        like(F32, TOKENS, 256),
        like(BF16, TOKENS, 384),
        like(F32, TOKENS, 128),
        like(BF16, TOKENS, 256),
    )
    return run(
        mixer_forward_kernel,
        "mixer_forward",
        outs,
        (core, *pieces, own, mate, rope, aux, segrow, pack),
        [SMEM] + [ANY] * 12 + [VMEM] * 2,
        [pltpu.VMEM(ROW, BF16), pltpu.VMEM((8, 2, 64, WIDE), BF16), held(rope), held(aux)]
        + [held(a) for a in outs[1:]]
        + [pltpu.SemaphoreType.DMA((n,)) for n in (12, 11)],
        FORWARD_US,
        [ANY] * 7,
    )


def mixer_backward(
    core, mix_grad, own, mate, normed, aux, segrow, pack, rope, proj, states, qkv, lse, second
):
    outs = (like(BF16, TOKENS, WIDTH), like(BF16, TOKENS, SENT), like(F32, 16, EARLY))
    moved = (qkv, lse, aux, rope, proj, states)
    return run(
        mixer_backward_kernel,
        "mixer_backward",
        outs,
        (core, mix_grad, own, mate, *moved, normed, segrow, pack, second),
        [SMEM] + [ANY] * 10 + [VMEM] * 3,
        [held(mix_grad), pltpu.VMEM((8, 2, 64, WIDE), BF16)]
        + [held(a) for a in moved]
        + [pltpu.VMEM(ROW, BF16)]
        + [held(a) for a in outs[0:2]]
        + [pltpu.VMEM((TOKENS, 256), F32), pltpu.VMEM((TOKENS, 256), F32)]
        + [pltpu.SemaphoreType.DMA((n,)) for n in (10, 5)],
        BACKWARD_US,
        [ANY] * 2 + [VMEM],
    )


def feed_forward_backward(core, normed, cot, weights):
    return run(
        feed_kernel,
        "feed",
        [like(BF16, *HERE)] * 8
        + [like(BF16, 512, 2 * FEED), like(BF16, 512, 4 * FEED), like(F32, 8, WIDTH)],
        (core, *normed, *cot, *weights),
        [SMEM] + [VMEM] * 8 + [ANY] * 2,
        [pltpu.VMEM((2, 8, 2, 64, 768), BF16), pltpu.SemaphoreType.DMA((2,))],
    )


def aux_arrays(seg):
    columns = [seg]
    for lag in range(1, 4):
        earlier = jnp.concatenate([jnp.full((lag,), -1.0, F32), seg[: TOKENS - lag]])
        columns.append((earlier == seg).astype(F32))
    ends = seg.reshape(BLOCKS, BLOCK)[:, -1]
    before = jnp.concatenate([jnp.full((1,), -1.0, F32), ends[:-1]])
    columns.append((seg == jnp.repeat(before, BLOCK)).astype(F32))
    columns.append((seg == jnp.repeat(ends, BLOCK)).astype(F32))
    aux = jnp.pad(jnp.stack(columns, axis=1), ((0, 8), (0, 128 - len(columns))))
    return (aux, jnp.broadcast_to(seg, (8, TOKENS)))


def rope_arrays():
    half = AHDIM // 2
    freq = (ROPE_BASE ** (-2.0 * np.arange(half) / AHDIM)).astype(np.float32)
    angles = np.arange(TOKENS, dtype=np.float32)[:, None] * freq[None, :]
    cosine, sine = (np.cos(angles.astype(np.float64)), np.sin(angles.astype(np.float64)))
    none = np.zeros_like(sine)
    parts = [cosine, cosine, none, none, -sine, none, none, none, none, sine, none, none]
    return jnp.asarray(np.concatenate(parts, axis=1).astype(np.float32))


def pad_columns(values, width, before=0):
    return jnp.pad(values, ((0, 0), (before, width - before - values.shape[1])))


def index_of(axes):
    return lax.axis_index(axes)


def exchange(values, axes, turn):
    size = 2 ** len(axes)
    return lax.ppermute(values, axes, [(i, turn(i)) for i in range(size)])


def other_core(values):
    return exchange(values, ("c",), lambda i: i ^ 1)


def near_gather(shard):
    return [shard] + near_return([shard] * 4)


def near_return(pieces):
    return [exchange(pieces[j], NEAR, lambda i, j=j: i ^ j) for j in range(1, 4)]


def spread_blocks(shard, axes):
    copies = jnp.broadcast_to(shard, (2 ** len(axes), *shard.shape))
    return turn_blocks(copies, axes)


def turn_blocks(blocks, axes):
    return lax.all_to_all(blocks, axes, split_axis=0, concat_axis=0, tiled=True)


def sum_blocks(blocks):
    return jnp.sum(blocks.astype(F32), axis=0)


def body(
    block_input,
    segments,
    first_gain,
    mamba_gate,
    mamba_input,
    step_weight,
    state_weight,
    conv_inner,
    conv_state,
    decay_log,
    step_bias,
    skip_scale,
    query_weight,
    keyval_weight,
    mamba_out,
    attention_out,
    second_gain,
    feed_gate,
    feed_up,
    feed_down,
    cotangent,
):
    kv_head = lax.axis_index("yh")
    core = jnp.stack([lax.axis_index("c"), kv_head, lax.axis_index(TENSOR)]).astype(jnp.int32)
    x, cot = (block_input[0], cotangent[0])
    gain_one, gain_two = (first_gain[None], second_gain[None])
    shared = spread_blocks(jnp.concatenate([state_weight, keyval_weight], axis=1), TENSOR)
    shared = shared.reshape(-1, 512)
    (normed_here,) = run(first_norm_kernel, "first_norm", [like(BF16, *HERE)], (x, gain_one))
    normed_pieces = [normed_here] + [
        exchange(normed_here, TENSOR, lambda i, k=k: i ^ k) for k in range(1, 8)
    ]
    pack = jnp.concatenate(
        [
            jnp.concatenate([conv_state, pad_columns(conv_inner, 256)], axis=1),
            jnp.zeros((4, 512), F32),
            pad_columns(step_bias[None], 512, STEP_LANE),
            pad_columns(decay_log[None], 512, STEP_LANE),
            pad_columns(jnp.repeat(skip_scale, HDIM)[None], 512),
            jnp.zeros((5, 512), F32),
        ],
        axis=0,
    )
    aux, segrow = aux_arrays(segments.reshape(TOKENS).astype(F32))
    rope = rope_arrays()

    feed_here = jnp.concatenate([feed_gate, feed_up, feed_down.T], axis=1)
    feed_copies = jnp.broadcast_to(feed_here, (16, *feed_here.shape))
    share_rows = shared.shape[0]
    key_part = lax.dynamic_slice(shared, (0, 256 + kv_head * AHDIM), (share_rows, AHDIM))
    value_part = lax.dynamic_slice(
        shared, (0, 256 + (KVHEADS + kv_head) * AHDIM), (share_rows, AHDIM)
    )
    main_here = jnp.concatenate(
        [
            shared[:, 0:256],
            key_part,
            value_part,
            query_weight,
            pad_columns(step_weight, 64),
            mamba_input,
            mamba_gate,
            mamba_out.T,
            attention_out.T,
        ],
        axis=1,
    )
    own = spread_blocks(main_here, CHIPS)
    mate = other_core(own)

    own, feed_copies, aux, segrow, pack = lax.optimization_barrier(
        (own, feed_copies, aux, segrow, pack)
    )
    feed_own = turn_blocks(feed_copies, FEED16).reshape(2, 8, share_rows, 768)

    normed, mix, proj, states, qkv, lse, heads = mixer_forward(
        core, normed_pieces, own, mate, aux, segrow, pack, rope
    )
    mix, feed_own, cot_here = lax.optimization_barrier((mix, feed_own, cot))
    feed_weights = (feed_own, other_core(feed_own))
    mix_blocks, *cot_pieces = lax.optimization_barrier(
        (turn_blocks(mix.reshape(ROW), TENSOR), *near_gather(cot_here))
    )
    hidden, normed_two_here = run(
        second_norm_kernel,
        "second_norm",
        [like(F32, *HERE), like(BF16, *HERE)],
        (x, gain_two, mix_blocks),
    )
    normed_two = near_gather(normed_two_here)
    *parts, act, feed_grads, second_part = feed_forward_backward(
        core, normed_two, cot_pieces, feed_weights
    )
    feed_keep, feed_send = run(
        feed_weights_kernel,
        "feed_weights",
        [like(BF16, 2, 8, share_rows, 768)] * 2,
        (core, *normed_two, *cot_pieces, act, feed_grads),
        [SMEM] + [VMEM] * 10,
        [pltpu.VMEM((2, 8, 2, 64, 768), BF16), pltpu.SemaphoreType.DMA((2,))],
        out_specs=[ANY] * 2,
    )
    sums = near_return(parts[4:8])
    hidden, feed_keep, feed_send, *sums = lax.optimization_barrier(
        (hidden, feed_keep, feed_send, *sums)
    )
    hidden_grad, mix_grad_copies = run(
        hidden_grad_kernel,
        "hidden_grad",
        [like(F32, *HERE), like(BF16, *ROW)],
        (hidden, gain_two, cot, parts[4], *sums),
    )
    (feed_pair,) = run(
        feed_pair_kernel,
        "feed_pair",
        [like(BF16, 2, 8, share_rows, 768)],
        (feed_keep, other_core(feed_send)),
    )
    mix_grad = turn_blocks(mix_grad_copies, TENSOR).reshape(TOKENS, WIDTH)
    feed_pair, mix_grad = lax.optimization_barrier((feed_pair, mix_grad))
    feed_blocks = turn_blocks(feed_pair.reshape(16, share_rows, 768), FEED16)

    normed_grad, dproj, small = mixer_backward(
        core, mix_grad, own, mate, normed, aux, segrow, pack, rope, proj, states, qkv, lse,
        second_part,
    )
    normed_grad, feed_blocks, *out_sums = lax.optimization_barrier(
        (normed_grad, feed_blocks, *near_return(parts[0:4]))
    )
    input_blocks = turn_blocks(normed_grad.reshape(ROW), TENSOR)
    keep, send = run(
        mixer_weights_kernel,
        "mixer_weights",
        [like(BF16, 8, share_rows, WIDE)] * 2,
        (core, normed, dproj, mix_grad, heads),
        [SMEM] + [VMEM] * 4,
        [pltpu.VMEM((8, 2, 64, WIDE), BF16), pltpu.SemaphoreType.DMA((2,))],
        out_specs=[ANY] * 2,
    )
    (pair,) = run(
        mixer_pair_kernel,
        "mixer_pair",
        [like(BF16, 8, share_rows + 16, WIDE)],
        (keep, other_core(send), small, other_core(small)),
    )
    pair, input_blocks = lax.optimization_barrier((pair, input_blocks))
    (block_out,) = run(
        output_kernel, "output", [like(BF16, *HERE)], (hidden, parts[0], *out_sums)
    )
    blocks = turn_blocks(pair, CHIPS)
    (input_grad,) = run(
        input_grad_kernel,
        "input_grad",
        [like(F32, *HERE)],
        (x, gain_one, hidden_grad, input_blocks),
    )
    feed_total = sum_blocks(feed_blocks)
    lines, gate_sum, input_sum, step_sum, query_sum, mamba_sum, attend_sum, own = run(
        collect_kernel,
        "collect",
        [
            like(F32, 8, 24, 512),
            like(F32, share_rows, INNER),
            like(F32, share_rows, INNER),
            like(F32, share_rows, HEADS),
            like(F32, share_rows, AHDIM),
            like(F32, INNER, share_rows),
            like(F32, AHDIM, share_rows),
            like(F32, 16, EARLY),
        ],
        (core, blocks),
        [SMEM, VMEM],
    )
    state_sum, keyval_sum, state_taps, first_sum, second_sum = run(
        last_kernel,
        "last",
        [
            like(F32, 8, 256),
            like(F32, 8, 256),
            like(F32, 4, 256),
            like(F32, 8, 128),
            like(F32, 8, 128),
        ],
        (turn_blocks(lines, TENSOR), first_gain.reshape(8, 128), second_gain.reshape(8, 128)),
    )
    return (
        block_out[None],
        input_grad[None],
        first_sum.reshape(-1),
        gate_sum,
        input_sum,
        step_sum,
        state_sum,
        own[4:8, 0:INNER],
        state_taps,
        own[8, 128 : 128 + HEADS],
        own[9, 128 : 128 + HEADS],
        jnp.sum(own[8, INNER : 2 * INNER].reshape(HEADS, HDIM), axis=1),
        query_sum,
        keyval_sum,
        mamba_sum,
        attend_sum,
        second_sum.reshape(-1),
        feed_total[:, 0:256],
        feed_total[:, 256:512],
        feed_total[:, 512:768].T,
    )


def solution(mesh):
    DP, TP = (("zlo", "xh", "xl", "c"), ("yh", "yl", "zhi"))
    fine = jax.sharding.Mesh(mesh.devices.reshape(FINE_SIZES), (*DP, *TP))
    in_specs = (
        P(DP, TP, None),
        P(DP, None),
        P(),
        P(DP, TP),
        P(DP, TP),
        P(DP, TP),
        P((*DP, *TP), None),
        P(None, TP),
        P(),
        P(TP),
        P(TP),
        P(TP),
        P(DP, TP),
        P((*DP, *TP), None),
        P(TP, DP),
        P(TP, DP),
        P(),
        P(DP, TP),
        P(DP, TP),
        P(TP, DP),
        P(DP, TP, None),
    )
    out_specs = (
        P(DP, TP, None),
        P(DP, TP, None),
        P(),
        P(DP, TP),
        P(DP, TP),
        P(DP, TP),
        P((*DP, *TP), None),
        P(None, TP),
        P(),
        P(TP),
        P(TP),
        P(TP),
        P(DP, TP),
        P((*DP, *TP), None),
        P(TP, DP),
        P(TP, DP),
        P(),
        P(DP, TP),
        P(DP, TP),
        P(TP, DP),
    )
    return jax.shard_map(body, mesh=fine, in_specs=in_specs, out_specs=out_specs, check_vma=False)
```

profile of v0, /device:TPU:0, one launch (start us, length us, event | category | flops | bytes accessed | tf_op | source)
XLA Modules:
  0.0 324.3 jit_solution(3861579948264101343)
XLA Ops:
  2.0 7.9 %all-to-all-start = ((bf16[8,8,512]{2,1,0:T(8,128)(2,1)}), bf16[8,8,512]{2,1,0:T(8,128)(2,1)S(1)}, u32[]{:S(2)}, u32[]{:S(2)}) async-start(bf16[8,8,512]{2,1,0:T(8,128)(2,1)} %broadcast_in_dim.47), calls=%async_computation | async-start | bytes 131072 | tf_op jit(solution)/shard_map/all_to_all | solution.py:854
  11.5 6.2 %all-to-all-done = bf16[8,8,512]{2,1,0:T(8,128)(2,1)S(1)} async-done(((bf16[8,8,512]{2,1,0:T(8,128)(2,1)}), bf16[8,8,512]{2,1,0:T(8,128)(2,1)S(1)}, u32[]{:S(2)}, u32[]{:S(2)}) %all-to-all-start) | async-done | bytes 65568 | tf_op jit(solution)/shard_map/all_to_all | solution.py:854
  19.9 4.9 %all-to-all-start.1 = ((bf16[8,64,1152]{2,1,0:T(8,128)(2,1)}), bf16[8,64,1152]{2,1,0:T(8,128)(2,1)S(1)}, u32[]{:S(2)}, u32[]{:S(2)}) async-start(bf16[8,64,1152]{2,1,0:T(8,128)(2,1)} %broadcast_in_dim.48), calls=%async_computation.1 | async-start | bytes 2359296 | tf_op jit(solution)/shard_map/all_to_all | solution.py:854
  24.8 1.8 first_norm.1.p0
  26.6 2.0 collective-permute-start.6
  28.6 2.1 collective-permute-start.5
  30.7 1.7 collective-permute-start.4
  32.4 3.4 %collective-permute-start.3 = (bf16[128,1024]{1,0:T(8,128)(2,1)}, bf16[128,1024]{1,0:T(8,128)(2,1)}, u32[]{:S(2)}, u32[]{:S(2)}) collective-permute-start(bf16[128,1024]{1,0:T(8,128)(2,1)} %first_norm.1.p0), channel_id=1, source_target_pairs={{0,4},{1,5},{2,6},{3,7},{4,0},{5,1},{6,2},{7,3},{8,12},{9,13},{10,... | collective-permute-start | bytes 786440 | tf_op jit(solution)/shard_map/ppermute | solution.py:833
  35.8 12.6 %all-to-all-done.1.own_hbm = bf16[8,64,1152]{2,1,0:T(8,128)(2,1)S(1)} async-done(((bf16[8,64,1152]{2,1,0:T(8,128)(2,1)}), bf16[8,64,1152]{2,1,0:T(8,128)(2,1)S(1)}, u32[]{:S(2)}, u32[]{:S(2)}) %all-to-all-start.1) | async-done | bytes 1179680 | tf_op jit(solution)/shard_map/all_to_all | solution.py:854
  49.1 4.7 %collective-permute-done.6.p7 = bf16[128,1024]{1,0:T(8,128)(2,1)S(1)} collective-permute-done((bf16[128,1024]{1,0:T(8,128)(2,1)}, bf16[128,1024]{1,0:T(8,128)(2,1)S(1)}, u32[]{:S(2)}, u32[]{:S(2)}) %collective-permute-start.6) | collective-permute-done | bytes 262176 | tf_op jit(solution)/shard_map/ppermute | solution.py:833
  53.9 1.6 collective-permute-done.5.p6
  56.6 2.3 collective-permute-start
  64.2 6.8 %all-to-all-start.2 = ((bf16[16,64,768]{2,1,0:T(8,128)(2,1)}), bf16[16,64,768]{2,1,0:T(8,128)(2,1)S(1)}, u32[]{:S(2)}, u32[]{:S(2)}) async-start(bf16[16,64,768]{2,1,0:T(8,128)(2,1)} %broadcast_in_dim.49), calls=%async_computation.2 | async-start | bytes 3145728 | tf_op jit(solution)/shard_map/all_to_all | solution.py:854
  71.0 15.1 %mixer_forward.1 = (bf16[8,128,1024]{2,1,0:T(8,128)(2,1)}, bf16[1024,1024]{1,0:T(8,128)(2,1)}, f32[1024,1024]{1,0:T(8,128)}, f32[1024,256]{1,0:T(8,128)}, bf16[1...) custom-call(s32[3]{0:T(128)} %pad_add_fusion.core_ref, bf16[128,1024]{1,0:T(8,128)(2,1)} %first_norm.1.p0, ...), custom_call_target="tpu_custom_call" | custom-call | flops 20000000000 | bytes 40000000 | tf_op jit(solution)/shard_map/mixer_forward/pallas_call | solution.py:717
  86.1 6.6 %all-to-all-done.2 = bf16[16,64,768]{2,1,0:T(8,128)(2,1)S(1)} async-done(((bf16[16,64,768]{2,1,0:T(8,128)(2,1)}), bf16[16,64,768]{2,1,0:T(8,128)(2,1)S(1)}, u32[]{:S(2)}, u32[]{:S(2)}) %all-to-all-start.2) | async-done | bytes 1572896 | tf_op jit(solution)/shard_map/all_to_all | solution.py:854
  93.8 4.9 %all-to-all-start.3 = ((bf16[8,128,1024]{2,1,0:T(8,128)(2,1)}), bf16[8,128,1024]{2,1,0:T(8,128)(2,1)S(1)}, u32[]{:S(2)}, u32[]{:S(2)}) async-start(bf16[8,128,1024]{2,1,0:T(8,128)(2,1)} %bitcast.64), calls=%async_computation.3 | async-start | bytes 4194304 | tf_op jit(solution)/shard_map/all_to_all | solution.py:854
  98.8 4.5 %collective-permute-start.10 = (bf16[128,1024]{1,0:T(8,128)(2,1)S(1)}, bf16[128,1024]{1,0:T(8,128)(2,1)S(1)}, u32[]{:S(2)}, u32[]{:S(2)}) collective-permute-start(bf16[128,1024]{1,0:T(8,128)(2,1)S(1)} %bitcast.60), channel_id=1, source_target_pairs={{0,3},{1,2},{2,1},{3,0},{4,7},{5,6},{6,5},{7,4},{8,11},{9,10},{10,... | collective-permute-start | bytes 786440 | tf_op jit(solution)/shard_map/ppermute | solution.py:833
  103.9 29.5 %collective-permute-done.10.c3 = bf16[128,1024]{1,0:T(8,128)(2,1)S(1)} collective-permute-done((bf16[128,1024]{1,0:T(8,128)(2,1)S(1)}, bf16[128,1024]{1,0:T(8,128)(2,1)S(1)}, u32[]{:S(2)}, u32[]{:S(2)}) %collective-permute-start.10) | collective-permute-done | bytes 262176 | tf_op jit(solution)/shard_map/ppermute | solution.py:833
  134.9 2.9 second_norm.1
  137.8 3.1 collective-permute-start.13
  140.9 1.7 collective-permute-start.12
  142.8 5.0 %collective-permute-done.13.n3 = bf16[128,1024]{1,0:T(8,128)(2,1)S(1)} collective-permute-done((bf16[128,1024]{1,0:T(8,128)(2,1)}, bf16[128,1024]{1,0:T(8,128)(2,1)S(1)}, u32[]{:S(2)}, u32[]{:S(2)}) %collective-permute-start.13) | collective-permute-done | bytes 262176 | tf_op jit(solution)/shard_map/ppermute | solution.py:833
  147.8 2.2 collective-permute-done.12.n2
  151.4 8.4 %feed.1 = (bf16[128,1024]{1,0:T(8,128)(2,1)}, bf16[128,1024]{1,0:T(8,128)(2,1)}, bf16[128,1024]{1,0:T(8,128)(2,1)}, bf16[128,1024]{1,0:T(8,128)(2,1)}, bf16[128,...) custom-call(s32[3]{0:T(128)} %pad_add_fusion.core_ref, ...), custom_call_target="tpu_custom_call" | custom-call | flops 50000000 | bytes 100000 | tf_op jit(solution)/shard_map/feed/pallas_call | solution.py:717
  159.8 2.3 collective-permute-start.15
  162.1 2.3 collective-permute-start.16
  165.1 5.5 %feed_weights.1 = (bf16[2,8,64,768]{3,2,1,0:T(8,128)(2,1)}, bf16[2,8,64,768]{3,2,1,0:T(8,128)(2,1)}) custom-call(s32[3]{0:T(128)} %pad_add_fusion.core_ref, bf16[128,1024]{1,0:T(8,128)(2,1)} %get-tuple-element.100.n0, bf16[128,1024]{1,0:T(8,128)(2,1)} %copy-done.13, bf16[128,1024]{1,0:T(8,128)(2,1)} %copy-done.12, bf16[128,1024]{1,0:T(8,128)(2,1)} %copy-done.11, ...), custom_call_target="tpu_custom_call" | custom-call | flops 50000000 | bytes 100000 | tf_op jit(solution)/shard_map/feed_weights/pallas_call | solution.py:717
  171.8 3.5 %collective-permute-done.17.s3 = bf16[128,1024]{1,0:T(8,128)(2,1)S(1)} collective-permute-done((bf16[128,1024]{1,0:T(8,128)(2,1)}, bf16[128,1024]{1,0:T(8,128)(2,1)S(1)}, u32[]{:S(2)}, u32[]{:S(2)}) %collective-permute-start.17) | collective-permute-done | bytes 262176 | tf_op jit(solution)/shard_map/ppermute | solution.py:833
  176.0 3.4 %hidden_grad.1 = (f32[128,1024]{1,0:T(8,128)}, bf16[8,128,1024]{2,1,0:T(8,128)(2,1)}) custom-call(f32[128,1024]{1,0:T(8,128)} %get-tuple-element.113.hidden_ref, f32[1,1024]{1,0:T(1,128)} %bitcast.76, bf16[128,1024]{1,0:T(8,128)(2,1)} %bitcast.59, bf16[128,1024]{1,0:T(8,128)(2,1)} %get-tuple-element.117.s0, bf16[128,1024]{1,0:T(8,128)(2,1)} %copy-done.17, ...), custom_call_target="tpu_custom_call" | custom-call | flops 50000000 | bytes 100000 | tf_op jit(solution)/shard_map/hidden_grad/pallas_call | solution.py:717
  179.3 7.2 %all-to-all-start.4 = ((bf16[8,128,1024]{2,1,0:T(8,128)(2,1)}), bf16[8,128,1024]{2,1,0:T(8,128)(2,1)S(1)}, u32[]{:S(2)}, u32[]{:S(2)}) async-start(bf16[8,128,1024]{2,1,0:T(8,128)(2,1)} %get-tuple-element.121), calls=%async_computation.4 | async-start | bytes 4194304 | tf_op jit(solution)/shard_map/all_to_all | solution.py:854
  186.6 3.5 %collective-permute-start.19 = (bf16[128,1024]{1,0:T(8,128)(2,1)}, bf16[128,1024]{1,0:T(8,128)(2,1)S(1)}, u32[]{:S(2)}, u32[]{:S(2)}) collective-permute-start(bf16[128,1024]{1,0:T(8,128)(2,1)} %get-tuple-element.131), channel_id=1, source_target_pairs={{0,1},{1,0},{2,3},{3,2},{4,5},{5,4},{6,7},{7,6},{8,9},{9,8},{10,11... | collective-permute-start | bytes 786440 | tf_op jit(solution)/shard_map/ppermute | solution.py:833
  191.7 3.4 %feed_pair.1 = bf16[2,8,64,768]{3,2,1,0:T(8,128)(2,1)} custom-call(bf16[2,8,64,768]{3,2,1,0:T(8,128)(2,1)} %get-tuple-element.115.keep_ref, bf16[2,8,64,768]{3,2,1,0:T(8,128)(2,1)} %collective-permute-done.18.come_ref), custom_call_target="tpu_custom_call" | custom-call | flops 50000000 | bytes 100000 | tf_op jit(solution)/shard_map/feed_pair/pallas_call | solution.py:717
  195.1 21.2 %all-to-all-done.4 = bf16[8,128,1024]{2,1,0:T(8,128)(2,1)S(1)} async-done(((bf16[8,128,1024]{2,1,0:T(8,128)(2,1)}), bf16[8,128,1024]{2,1,0:T(8,128)(2,1)S(1)}, u32[]{:S(2)}, u32[]{:S(2)}) %all-to-all-start.4) | async-done | bytes 2097184 | tf_op jit(solution)/shard_map/all_to_all | solution.py:854
  217.6 6.1 %all-to-all-start.5 = ((bf16[16,64,768]{2,1,0:T(8,128)(2,1)}), bf16[16,64,768]{2,1,0:T(8,128)(2,1)}, u32[]{:S(2)}, u32[]{:S(2)}) async-start(bf16[16,64,768]{2,1,0:T(8,128)(2,1)} %bitcast.53), calls=%async_computation.5 | async-start | bytes 3145728 | tf_op jit(solution)/shard_map/all_to_all | solution.py:854
  223.7 26.5 %mixer_backward.1 = (bf16[1024,1024]{1,0:T(8,128)(2,1)}, bf16[1024,896]{1,0:T(8,128)(2,1)}, f32[16,384]{1,0:T(8,128)}) custom-call(s32[3]{0:T(128)} %pad_add_fusion.core_ref, bf16[1024,1024]{1,0:T(8,128)(2,1)} %bitcast.49, bf16[8,64,1152]{2,1,0:T(8,128)(2,1)} %copy-done.6, bf16[8,64,1152]{2,1,0:T(8,128)(2,1)} %collective-permute-done.7.mate_hbm, ...), custom_call_target="tpu_custom_call" | custom-call | flops 32999999488 | bytes 66000000 | tf_op jit(solution)/shard_map/mixer_backward/pallas_call | solution.py:717
  251.1 6.0 %all-to-all-start.6 = ((bf16[8,128,1024]{2,1,0:T(8,128)(2,1)}), bf16[8,128,1024]{2,1,0:T(8,128)(2,1)S(1)}, u32[]{:S(2)}, u32[]{:S(2)}) async-start(bf16[8,128,1024]{2,1,0:T(8,128)(2,1)} %bitcast.63), calls=%async_computation.6 | async-start | bytes 4194304 | tf_op jit(solution)/shard_map/all_to_all | solution.py:854
  257.1 7.3 %mixer_weights.1 = (bf16[8,64,1152]{2,1,0:T(8,128)(2,1)}, bf16[8,64,1152]{2,1,0:T(8,128)(2,1)}) custom-call(s32[3]{0:T(128)} %pad_add_fusion.core_ref, bf16[8,128,1024]{2,1,0:T(8,128)(2,1)} %get-tuple-element.127.normed_hbm.normed_ref, bf16[1024,896]{1,0:T(8,128)(2,1)} %get-tuple-element.138.dproj_ref, bf16[1024,1024]{1,0:T(8,128)(2,1)} %bitcast.50, ...), custom_call_target="tpu_custom_call" | custom-call | flops 50000000 | bytes 100000 | tf_op jit(solution)/shard_map/mixer_weights/pallas_call | solution.py:717
  265.0 2.0 collective-permute-done.23.small_come_ref
  268.6 3.0 mixer_pair.1
  271.6 9.9 %all-to-all-done.6.blocks_ref = bf16[8,128,1024]{2,1,0:T(8,128)(2,1)S(1)} async-done(((bf16[8,128,1024]{2,1,0:T(8,128)(2,1)}), bf16[8,128,1024]{2,1,0:T(8,128)(2,1)S(1)}, u32[]{:S(2)}, u32[]{:S(2)}) %all-to-all-start.6) | async-done | bytes 2097184 | tf_op jit(solution)/shard_map/all_to_all | solution.py:854
  281.5 4.6 %all-to-all-start.7 = ((bf16[8,80,1152]{2,1,0:T(8,128)(2,1)}), bf16[8,80,1152]{2,1,0:T(8,128)(2,1)}, u32[]{:S(2)}, u32[]{:S(2)}) async-start(bf16[8,80,1152]{2,1,0:T(8,128)(2,1)} %mixer_pair.1), calls=%async_computation.7 | async-start | bytes 2949120 | tf_op jit(solution)/shard_map/all_to_all | solution.py:854
  286.1 1.6 convert_reduce_fusion
  288.4 15.1 %all-to-all-done.7.blocks_ref = bf16[8,80,1152]{2,1,0:T(8,128)(2,1)} async-done(((bf16[8,80,1152]{2,1,0:T(8,128)(2,1)}), bf16[8,80,1152]{2,1,0:T(8,128)(2,1)}, u32[]{:S(2)}, u32[]{:S(2)}) %all-to-all-start.7) | async-done | bytes 1474592 | tf_op jit(solution)/shard_map/all_to_all | solution.py:854
  303.5 2.4 collect.1
  305.9 5.3 %all-to-all-start.8 = ((f32[8,24,512]{2,1,0:T(8,128)}), f32[8,24,512]{2,1,0:T(8,128)S(1)}, u32[]{:S(2)}, u32[]{:S(2)}) async-start(f32[8,24,512]{2,1,0:T(8,128)} %get-tuple-element.146), calls=%async_computation.8 | async-start | bytes 786432 | tf_op jit(solution)/shard_map/all_to_all | solution.py:854
  311.2 2.2 output.1
  313.4 3.1 input_grad.1
  322.7 1.6 last.1
  (153 shorter events, 32.4 us)
Async XLA Ops:
  2.0 15.6 %all-to-all-start = ((bf16[8,8,512]{2,1,0:T(8,128)(2,1)}), bf16[8,8,512]{2,1,0:T(8,128)(2,1)S(1)}, u32[]{:S(2)}, u32[]{:S(2)}) async-start(bf16[8,8,512]{2,1,0:T(8,128)(2,1)} %broadcast_in_dim.47), calls=%async_computation | async-start | bytes 131072 | tf_op jit(solution)/shard_map/all_to_all | solution.py:854
  19.8 28.6 %copy-start.27 = (s32[1,1024]{1,0:T(1,128)S(1)}, s32[1,1024]{1,0:T(1,128)}, u32[]{:S(2)}) copy-start(s32[1,1024]{1,0:T(1,128)} %param.23) | copy-start | bytes 12292
  19.8 39.1 %copy-start.28 = (f32[4,192]{1,0:T(4,128)S(1)}, f32[4,192]{1,0:T(4,128)}, u32[]{:S(2)}) copy-start(f32[4,192]{1,0:T(4,128)} %param.29) | copy-start | bytes 9220
  19.8 39.1 %copy-start.29 = (f32[4,256]{1,0:T(4,128)S(1)}, f32[4,256]{1,0:T(4,128)}, u32[]{:S(2)}) copy-start(f32[4,256]{1,0:T(4,128)} %param.30) | copy-start | bytes 12292
  19.8 39.1 %copy-start.31 = (f32[3]{0:T(128)S(1)}, f32[3]{0:T(128)}, u32[]{:S(2)}) copy-start(f32[3]{0:T(128)} %param.31) | copy-start | bytes 40
  19.8 39.2 %copy-start.32 = (f32[3]{0:T(128)S(1)}, f32[3]{0:T(128)}, u32[]{:S(2)}) copy-start(f32[3]{0:T(128)} %param.32) | copy-start | bytes 40
  19.8 39.2 %copy-start.30 = (f32[3]{0:T(128)S(1)}, f32[3]{0:T(128)}, u32[]{:S(2)}) copy-start(f32[3]{0:T(128)} %param.33) | copy-start | bytes 40
  19.9 28.6 %all-to-all-start.1 = ((bf16[8,64,1152]{2,1,0:T(8,128)(2,1)}), bf16[8,64,1152]{2,1,0:T(8,128)(2,1)S(1)}, u32[]{:S(2)}, u32[]{:S(2)}) async-start(bf16[8,64,1152]{2,1,0:T(8,128)(2,1)} %broadcast_in_dim.48), calls=%async_computation.1 | async-start | bytes 2359296 | tf_op jit(solution)/shard_map/all_to_all | solution.py:854
  24.8 37.5 %copy-start.22 = (bf16[256,64]{0,1:T(8,128)(2,1)S(1)}, bf16[256,64]{0,1:T(8,128)(2,1)}, u32[]{:S(2)}) copy-start(bf16[256,64]{0,1:T(8,128)(2,1)} %param.41) | copy-start | bytes 98308
  24.8 37.5 %copy-start.23 = (bf16[64,256]{1,0:T(8,128)(2,1)S(1)}, bf16[64,256]{1,0:T(8,128)(2,1)}, u32[]{:S(2)}) copy-start(bf16[64,256]{1,0:T(8,128)(2,1)} %param.40) | copy-start | bytes 98308
  24.8 37.5 %copy-start.24 = (bf16[64,256]{1,0:T(8,128)(2,1)S(1)}, bf16[64,256]{1,0:T(8,128)(2,1)}, u32[]{:S(2)}) copy-start(bf16[64,256]{1,0:T(8,128)(2,1)} %param.39) | copy-start | bytes 98308
  26.6 27.3 %collective-permute-start.6 = (bf16[128,1024]{1,0:T(8,128)(2,1)}, bf16[128,1024]{1,0:T(8,128)(2,1)S(1)}, u32[]{:S(2)}, u32[]{:S(2)}) collective-permute-start(bf16[128,1024]{1,0:T(8,128)(2,1)} %first_norm.1.p0), channel_id=1, source_target_pairs={{0,7},{1,6},{2,5},{3,4},{4,3},{5,2},{6,1},{7,0},{8,15},{9,14},{10,... | collective-permute-start | bytes 786440 | tf_op jit(solution)/shard_map/ppermute | solution.py:833
  28.6 26.8 %collective-permute-start.5 = (bf16[128,1024]{1,0:T(8,128)(2,1)}, bf16[128,1024]{1,0:T(8,128)(2,1)S(1)}, u32[]{:S(2)}, u32[]{:S(2)}) collective-permute-start(bf16[128,1024]{1,0:T(8,128)(2,1)} %first_norm.1.p0), channel_id=1, source_target_pairs={{0,6},{1,7},{2,4},{3,5},{4,2},{5,3},{6,0},{7,1},{8,14},{9,15},{10,... | collective-permute-start | bytes 786440 | tf_op jit(solution)/shard_map/ppermute | solution.py:833
  30.7 25.9 %collective-permute-start.4 = (bf16[128,1024]{1,0:T(8,128)(2,1)}, bf16[128,1024]{1,0:T(8,128)(2,1)S(1)}, u32[]{:S(2)}, u32[]{:S(2)}) collective-permute-start(bf16[128,1024]{1,0:T(8,128)(2,1)} %first_norm.1.p0), channel_id=1, source_target_pairs={{0,5},{1,4},{2,7},{3,6},{4,1},{5,0},{6,3},{7,2},{8,13},{9,12},{10,... | collective-permute-start | bytes 786440 | tf_op jit(solution)/shard_map/ppermute | solution.py:833
  32.4 38.6 %collective-permute-start.3 = (bf16[128,1024]{1,0:T(8,128)(2,1)}, bf16[128,1024]{1,0:T(8,128)(2,1)}, u32[]{:S(2)}, u32[]{:S(2)}) collective-permute-start(bf16[128,1024]{1,0:T(8,128)(2,1)} %first_norm.1.p0), channel_id=1, source_target_pairs={{0,4},{1,5},{2,6},{3,7},{4,0},{5,1},{6,2},{7,3},{8,12},{9,13},{10,... | collective-permute-start | bytes 786440 | tf_op jit(solution)/shard_map/ppermute | solution.py:833
  48.4 15.7 %copy-start.6 = (bf16[8,64,1152]{2,1,0:T(8,128)(2,1)}, bf16[8,64,1152]{2,1,0:T(8,128)(2,1)S(1)}, u32[]{:S(2)}) copy-start(bf16[8,64,1152]{2,1,0:T(8,128)(2,1)S(1)} %all-to-all-done.1.own_hbm) | copy-start | bytes 3538948
  48.4 22.6 %collective-permute-start.7 = (bf16[8,64,1152]{2,1,0:T(8,128)(2,1)S(1)}, bf16[8,64,1152]{2,1,0:T(8,128)(2,1)}, u32[]{:S(2)}, u32[]{:S(2)}) collective-permute-start(bf16[8,64,1152]{2,1,0:T(8,128)(2,1)S(1)} %all-to-all-done.1.own_hbm), channel_id=1, source_target_pairs={{0,8},{8,0},{1,9},{9,1},{2,10},{10,2},{3,11},{11,3},{4,12},{12,4},... | collective-permute-start | bytes 3538952 | tf_op jit(solution)/shard_map/ppermute | solution.py:833
  53.9 17.1 %collective-permute-start.2 = (bf16[128,1024]{1,0:T(8,128)(2,1)}, bf16[128,1024]{1,0:T(8,128)(2,1)}, u32[]{:S(2)}, u32[]{:S(2)}) collective-permute-start(bf16[128,1024]{1,0:T(8,128)(2,1)} %first_norm.1.p0), channel_id=1, source_target_pairs={{0,3},{1,2},{2,1},{3,0},{4,7},{5,6},{6,5},{7,4},{8,11},{9,10},{10,... | collective-permute-start | bytes 786440 | tf_op jit(solution)/shard_map/ppermute | solution.py:833
  55.5 15.5 %collective-permute-start.1 = (bf16[128,1024]{1,0:T(8,128)(2,1)}, bf16[128,1024]{1,0:T(8,128)(2,1)}, u32[]{:S(2)}, u32[]{:S(2)}) collective-permute-start(bf16[128,1024]{1,0:T(8,128)(2,1)} %first_norm.1.p0), channel_id=1, source_target_pairs={{0,2},{1,3},{2,0},{3,1},{4,6},{5,7},{6,4},{7,5},{8,10},{9,11},{10,... | collective-permute-start | bytes 786440 | tf_op jit(solution)/shard_map/ppermute | solution.py:833
  56.6 14.3 %collective-permute-start = (bf16[128,1024]{1,0:T(8,128)(2,1)}, bf16[128,1024]{1,0:T(8,128)(2,1)}, u32[]{:S(2)}, u32[]{:S(2)}) collective-permute-start(bf16[128,1024]{1,0:T(8,128)(2,1)} %first_norm.1.p0), channel_id=1, source_target_pairs={{0,1},{1,0},{2,3},{3,2},{4,5},{5,4},{6,7},{7,6},{8,9},{9,8},{10,11... | collective-permute-start | bytes 786440 | tf_op jit(solution)/shard_map/ppermute | solution.py:833
  64.2 28.5 %all-to-all-start.2 = ((bf16[16,64,768]{2,1,0:T(8,128)(2,1)}), bf16[16,64,768]{2,1,0:T(8,128)(2,1)S(1)}, u32[]{:S(2)}, u32[]{:S(2)}) async-start(bf16[16,64,768]{2,1,0:T(8,128)(2,1)} %broadcast_in_dim.49), calls=%async_computation.2 | async-start | bytes 3145728 | tf_op jit(solution)/shard_map/all_to_all | solution.py:854
  93.8 39.7 %all-to-all-start.3 = ((bf16[8,128,1024]{2,1,0:T(8,128)(2,1)}), bf16[8,128,1024]{2,1,0:T(8,128)(2,1)S(1)}, u32[]{:S(2)}, u32[]{:S(2)}) async-start(bf16[8,128,1024]{2,1,0:T(8,128)(2,1)} %bitcast.64), calls=%async_computation.3 | async-start | bytes 4194304 | tf_op jit(solution)/shard_map/all_to_all | solution.py:854
  98.7 44.1 %collective-permute-start.14 = (bf16[2,8,64,768]{3,2,1,0:T(8,128)(2,1)}, bf16[2,8,64,768]{3,2,1,0:T(8,128)(2,1)}, u32[]{:S(2)}, u32[]{:S(2)}) collective-permute-start(bf16[2,8,64,768]{3,2,1,0:T(8,128)(2,1)} %bitcast.51), channel_id=1, source_target_pairs={{0,8},{8,0},{1,9},{9,1},{2,10},{10,2},{3,11},{11,3},{4,12},{12,4},... | collective-permute-start | bytes 4718600 | tf_op jit(solution)/shard_map/ppermute | solution.py:833
  98.8 34.7 %collective-permute-start.10 = (bf16[128,1024]{1,0:T(8,128)(2,1)S(1)}, bf16[128,1024]{1,0:T(8,128)(2,1)S(1)}, u32[]{:S(2)}, u32[]{:S(2)}) collective-permute-start(bf16[128,1024]{1,0:T(8,128)(2,1)S(1)} %bitcast.60), channel_id=1, source_target_pairs={{0,3},{1,2},{2,1},{3,0},{4,7},{5,6},{6,5},{7,4},{8,11},{9,10},{10,... | collective-permute-start | bytes 786440 | tf_op jit(solution)/shard_map/ppermute | solution.py:833
  103.3 30.2 %collective-permute-start.9 = (bf16[128,1024]{1,0:T(8,128)(2,1)S(1)}, bf16[128,1024]{1,0:T(8,128)(2,1)S(1)}, u32[]{:S(2)}, u32[]{:S(2)}) collective-permute-start(bf16[128,1024]{1,0:T(8,128)(2,1)S(1)} %bitcast.61), channel_id=1, source_target_pairs={{0,2},{1,3},{2,0},{3,1},{4,6},{5,7},{6,4},{7,5},{8,10},{9,11},{10,... | collective-permute-start | bytes 786440 | tf_op jit(solution)/shard_map/ppermute | solution.py:833
  103.8 29.6 %collective-permute-start.8 = (bf16[128,1024]{1,0:T(8,128)(2,1)S(1)}, bf16[128,1024]{1,0:T(8,128)(2,1)S(1)}, u32[]{:S(2)}, u32[]{:S(2)}) collective-permute-start(bf16[128,1024]{1,0:T(8,128)(2,1)S(1)} %bitcast.62), channel_id=1, source_target_pairs={{0,1},{1,0},{2,3},{3,2},{4,5},{5,4},{6,7},{7,6},{8,9},{9,8},{10,11... | collective-permute-start | bytes 786440 | tf_op jit(solution)/shard_map/ppermute | solution.py:833
  133.4 17.3 %copy-start.8 = (bf16[128,1024]{1,0:T(8,128)(2,1)}, bf16[128,1024]{1,0:T(8,128)(2,1)S(1)}, u32[]{:S(2)}) copy-start(bf16[128,1024]{1,0:T(8,128)(2,1)S(1)} %collective-permute-done.10.c3) | copy-start | bytes 786436
  133.4 17.3 %copy-start.9 = (bf16[128,1024]{1,0:T(8,128)(2,1)}, bf16[128,1024]{1,0:T(8,128)(2,1)S(1)}, u32[]{:S(2)}) copy-start(bf16[128,1024]{1,0:T(8,128)(2,1)S(1)} %collective-permute-done.9.c2) | copy-start | bytes 786436
  133.4 17.3 %copy-start.10 = (bf16[128,1024]{1,0:T(8,128)(2,1)}, bf16[128,1024]{1,0:T(8,128)(2,1)S(1)}, u32[]{:S(2)}) copy-start(bf16[128,1024]{1,0:T(8,128)(2,1)S(1)} %collective-permute-done.8.c1) | copy-start | bytes 786436
  137.8 10.0 %collective-permute-start.13 = (bf16[128,1024]{1,0:T(8,128)(2,1)}, bf16[128,1024]{1,0:T(8,128)(2,1)S(1)}, u32[]{:S(2)}, u32[]{:S(2)}) collective-permute-start(bf16[128,1024]{1,0:T(8,128)(2,1)} %get-tuple-element.100.n0), channel_id=1, source_target_pairs={{0,3},{1,2},{2,1},{3,0},{4,7},{5,6},{6,5},{7,4},{8,11},{9,10},{10,... | collective-permute-start | bytes 786440 | tf_op jit(solution)/shard_map/ppermute | solution.py:833
  140.9 9.1 %collective-permute-start.12 = (bf16[128,1024]{1,0:T(8,128)(2,1)}, bf16[128,1024]{1,0:T(8,128)(2,1)S(1)}, u32[]{:S(2)}, u32[]{:S(2)}) collective-permute-start(bf16[128,1024]{1,0:T(8,128)(2,1)} %get-tuple-element.100.n0), channel_id=1, source_target_pairs={{0,2},{1,3},{2,0},{3,1},{4,6},{5,7},{6,4},{7,5},{8,10},{9,11},{10,... | collective-permute-start | bytes 786440 | tf_op jit(solution)/shard_map/ppermute | solution.py:833
  142.6 8.1 %collective-permute-start.11 = (bf16[128,1024]{1,0:T(8,128)(2,1)}, bf16[128,1024]{1,0:T(8,128)(2,1)S(1)}, u32[]{:S(2)}, u32[]{:S(2)}) collective-permute-start(bf16[128,1024]{1,0:T(8,128)(2,1)} %get-tuple-element.100.n0), channel_id=1, source_target_pairs={{0,1},{1,0},{2,3},{3,2},{4,5},{5,4},{6,7},{7,6},{8,9},{9,8},{10,11... | collective-permute-start | bytes 786440 | tf_op jit(solution)/shard_map/ppermute | solution.py:833
  159.8 10.9 %collective-permute-start.15 = (bf16[128,1024]{1,0:T(8,128)(2,1)}, bf16[128,1024]{1,0:T(8,128)(2,1)S(1)}, u32[]{:S(2)}, u32[]{:S(2)}) collective-permute-start(bf16[128,1024]{1,0:T(8,128)(2,1)} %get-tuple-element.110), channel_id=1, source_target_pairs={{0,1},{1,0},{2,3},{3,2},{4,5},{5,4},{6,7},{7,6},{8,9},{9,8},{10,11... | collective-permute-start | bytes 786440 | tf_op jit(solution)/shard_map/ppermute | solution.py:833
  162.1 9.7 %collective-permute-start.16 = (bf16[128,1024]{1,0:T(8,128)(2,1)}, bf16[128,1024]{1,0:T(8,128)(2,1)S(1)}, u32[]{:S(2)}, u32[]{:S(2)}) collective-permute-start(bf16[128,1024]{1,0:T(8,128)(2,1)} %get-tuple-element.111), channel_id=1, source_target_pairs={{0,2},{1,3},{2,0},{3,1},{4,6},{5,7},{6,4},{7,5},{8,10},{9,11},{10,... | collective-permute-start | bytes 786440 | tf_op jit(solution)/shard_map/ppermute | solution.py:833
  164.4 10.9 %collective-permute-start.17 = (bf16[128,1024]{1,0:T(8,128)(2,1)}, bf16[128,1024]{1,0:T(8,128)(2,1)S(1)}, u32[]{:S(2)}, u32[]{:S(2)}) collective-permute-start(bf16[128,1024]{1,0:T(8,128)(2,1)} %get-tuple-element.112), channel_id=1, source_target_pairs={{0,3},{1,2},{2,1},{3,0},{4,7},{5,6},{6,5},{7,4},{8,11},{9,10},{10,... | collective-permute-start | bytes 786440 | tf_op jit(solution)/shard_map/ppermute | solution.py:833
  179.3 10.8 %copy-start.37 = (bf16[128,1024]{1,0:T(8,128)(2,1)S(1)}, bf16[128,1024]{1,0:T(8,128)(2,1)}, u32[]{:S(2)}) copy-start(bf16[128,1024]{1,0:T(8,128)(2,1)} %get-tuple-element.132) | copy-start | bytes 786436
  179.3 12.2 %copy-start.36 = (bf16[128,1024]{1,0:T(8,128)(2,1)S(1)}, bf16[128,1024]{1,0:T(8,128)(2,1)}, u32[]{:S(2)}) copy-start(bf16[128,1024]{1,0:T(8,128)(2,1)} %get-tuple-element.133) | copy-start | bytes 786436
  179.3 36.9 %all-to-all-start.4 = ((bf16[8,128,1024]{2,1,0:T(8,128)(2,1)}), bf16[8,128,1024]{2,1,0:T(8,128)(2,1)S(1)}, u32[]{:S(2)}, u32[]{:S(2)}) async-start(bf16[8,128,1024]{2,1,0:T(8,128)(2,1)} %get-tuple-element.121), calls=%async_computation.4 | async-start | bytes 4194304 | tf_op jit(solution)/shard_map/all_to_all | solution.py:854
  186.6 5.1 %collective-permute-start.18 = (bf16[2,8,64,768]{3,2,1,0:T(8,128)(2,1)}, bf16[2,8,64,768]{3,2,1,0:T(8,128)(2,1)}, u32[]{:S(2)}, u32[]{:S(2)}) collective-permute-start(bf16[2,8,64,768]{3,2,1,0:T(8,128)(2,1)} %get-tuple-element.116), channel_id=1, source_target_pairs={{0,8},{8,0},{1,9},{9,1},{2,10},{10,2},{3,11},{11,3},{4,12},{12,4},... | collective-permute-start | bytes 4718600 | tf_op jit(solution)/shard_map/ppermute | solution.py:833
  186.6 63.7 %collective-permute-start.19 = (bf16[128,1024]{1,0:T(8,128)(2,1)}, bf16[128,1024]{1,0:T(8,128)(2,1)S(1)}, u32[]{:S(2)}, u32[]{:S(2)}) collective-permute-start(bf16[128,1024]{1,0:T(8,128)(2,1)} %get-tuple-element.131), channel_id=1, source_target_pairs={{0,1},{1,0},{2,3},{3,2},{4,5},{5,4},{6,7},{7,6},{8,9},{9,8},{10,11... | collective-permute-start | bytes 786440 | tf_op jit(solution)/shard_map/ppermute | solution.py:833
  190.1 60.2 %collective-permute-start.20 = (bf16[128,1024]{1,0:T(8,128)(2,1)S(1)}, bf16[128,1024]{1,0:T(8,128)(2,1)S(1)}, u32[]{:S(2)}, u32[]{:S(2)}) collective-permute-start(bf16[128,1024]{1,0:T(8,128)(2,1)S(1)} %copy-done.37), channel_id=1, source_target_pairs={{0,2},{1,3},{2,0},{3,1},{4,6},{5,7},{6,4},{7,5},{8,10},{9,11},{10,... | collective-permute-start | bytes 786440 | tf_op jit(solution)/shard_map/ppermute | solution.py:833
  191.6 58.7 %collective-permute-start.21 = (bf16[128,1024]{1,0:T(8,128)(2,1)S(1)}, bf16[128,1024]{1,0:T(8,128)(2,1)S(1)}, u32[]{:S(2)}, u32[]{:S(2)}) collective-permute-start(bf16[128,1024]{1,0:T(8,128)(2,1)S(1)} %copy-done.36), channel_id=1, source_target_pairs={{0,3},{1,2},{2,1},{3,0},{4,7},{5,6},{6,5},{7,4},{8,11},{9,10},{10,... | collective-permute-start | bytes 786440 | tf_op jit(solution)/shard_map/ppermute | solution.py:833
  217.6 32.7 %all-to-all-start.5 = ((bf16[16,64,768]{2,1,0:T(8,128)(2,1)}), bf16[16,64,768]{2,1,0:T(8,128)(2,1)}, u32[]{:S(2)}, u32[]{:S(2)}) async-start(bf16[16,64,768]{2,1,0:T(8,128)(2,1)} %bitcast.53), calls=%async_computation.5 | async-start | bytes 3145728 | tf_op jit(solution)/shard_map/all_to_all | solution.py:854
  251.1 30.4 %all-to-all-start.6 = ((bf16[8,128,1024]{2,1,0:T(8,128)(2,1)}), bf16[8,128,1024]{2,1,0:T(8,128)(2,1)S(1)}, u32[]{:S(2)}, u32[]{:S(2)}) async-start(bf16[8,128,1024]{2,1,0:T(8,128)(2,1)} %bitcast.63), calls=%async_computation.6 | async-start | bytes 4194304 | tf_op jit(solution)/shard_map/all_to_all | solution.py:854
  264.4 3.2 collective-permute-start.22
  264.5 2.5 collective-permute-start.23
  281.5 22.0 %all-to-all-start.7 = ((bf16[8,80,1152]{2,1,0:T(8,128)(2,1)}), bf16[8,80,1152]{2,1,0:T(8,128)(2,1)}, u32[]{:S(2)}, u32[]{:S(2)}) async-start(bf16[8,80,1152]{2,1,0:T(8,128)(2,1)} %mixer_pair.1), calls=%async_computation.7 | async-start | bytes 2949120 | tf_op jit(solution)/shard_map/all_to_all | solution.py:854
  305.9 16.1 %all-to-all-start.8 = ((f32[8,24,512]{2,1,0:T(8,128)}), f32[8,24,512]{2,1,0:T(8,128)S(1)}, u32[]{:S(2)}, u32[]{:S(2)}) async-start(f32[8,24,512]{2,1,0:T(8,128)} %get-tuple-element.146), calls=%async_computation.8 | async-start | bytes 786432 | tf_op jit(solution)/shard_map/all_to_all | solution.py:854
  (23 other events, 80.4 us)
where the time goes:
time: 326 us; the launch traced here: 324 us
  waiting for transfers between devices  123 us (38%)
  starting transfers between devices  87.4 us (27%)
  Pallas kernels  86.6 us (27%)
  local copies, waits for them, and re-layouts  22.9 us (7%)
  other arithmetic  3.81 us (1%)
    pallas_call x14, Pallas kernels, run(): pl.pallas_call(kernel, in_specs=specs or [VMEM] * len(args), out_specs=ou...  86.6 us
    all_to_all x9, waiting for transfers between devices, turn_blocks(): return lax.all_to_all(blocks, axes, split_axis=0, concat_axis=0, tiled=True)  71.6 us
    all_to_all x9, starting transfers between devices, turn_blocks(): return lax.all_to_all(blocks, axes, split_axis=0, concat_axis=0, tiled=True)  53.7 us
    ppermute x24, waiting for transfers between devices, exchange(): return lax.ppermute(values, axes, [(i, turn(i)) for i in range(size)])  50.9 us
    ppermute x24, starting transfers between devices, exchange(): return lax.ppermute(values, axes, [(i, turn(i)) for i in range(size)])  33.7 us
    unnamed x81, local copies, waits for them, and re-layouts  10.3 us
  transfers between devices with their start and end apart: 33, of which 16 were waited for; matrix products, arithmetic and copies ran while one was open for 5% of the time, Pallas kernels for 22%

commit v1 on v0

--- a/solution.py
+++ b/solution.py
@@ -891,6 +891,7 @@
     normed_pieces = [normed_here] + [
         exchange(normed_here, TENSOR, lambda i, k=k: i ^ k) for k in range(1, 8)
     ]
+    shared, _ = lax.optimization_barrier((shared, normed_here))
     pack = jnp.concatenate(
         [
             jnp.concatenate([conv_state, pad_columns(conv_inner, 256)], axis=1),
@@ -1016,6 +1017,10 @@
         (x, gain_one, hidden_grad, input_blocks),
     )
     feed_total = sum_blocks(feed_blocks)
+    feed_outs = (feed_total[:, 0:256], feed_total[:, 256:512], feed_total[:, 512:768].T)
+    blocks, input_grad, block_out, *feed_outs = lax.optimization_barrier(
+        (blocks, input_grad, block_out, *feed_outs)
+    )
     lines, gate_sum, input_sum, step_sum, query_sum, mamba_sum, attend_sum, own = run(
         collect_kernel,
         "collect",
@@ -1062,9 +1067,7 @@
         mamba_sum,
         attend_sum,
         second_sum.reshape(-1),
-        feed_total[:, 0:256],
-        feed_total[:, 256:512],
-        feed_total[:, 512:768].T,
+        *feed_outs,
     )
 
 

time: 326 us -> 324 us (level)
  waiting for transfers between devices: 123 us -> 119 us
    unnamed x81 -> x79, local copies, waits for them, and re-layouts: 10.3 us -> 12 us
  transfers between devices with their start and end apart: 33 -> 33, of which waited for: 16 -> 17; matrix products, arithmetic and copies ran while one was open for 5% -> 5% of each run, Pallas kernels for 22% -> 22%
where the time goes in v1:
time: 324 us; the launch traced here: 322 us
  waiting for transfers between devices  119 us (37%)
  starting transfers between devices  87.2 us (27%)
  Pallas kernels  86.6 us (27%)
  local copies, waits for them, and re-layouts  24.6 us (8%)
  other arithmetic  3.81 us (1%)
    pallas_call x14, Pallas kernels, run(): pl.pallas_call(kernel, in_specs=specs or [VMEM] * len(args), out_specs=ou...  86.6 us
    all_to_all x9, waiting for transfers between devices, turn_blocks(): return lax.all_to_all(blocks, axes, split_axis=0, concat_axis=0, tiled=True)  68.5 us
    all_to_all x9, starting transfers between devices, turn_blocks(): return lax.all_to_all(blocks, axes, split_axis=0, concat_axis=0, tiled=True)  53.8 us
    ppermute x24, waiting for transfers between devices, exchange(): return lax.ppermute(values, axes, [(i, turn(i)) for i in range(size)])  50.6 us
    ppermute x24, starting transfers between devices, exchange(): return lax.ppermute(values, axes, [(i, turn(i)) for i in range(size)])  33.4 us
    unnamed x79, local copies, waits for them, and re-layouts  12 us
  transfers between devices with their start and end apart: 33, of which 17 were waited for; matrix products, arithmetic and copies ran while one was open for 5% of the time, Pallas kernels for 22%

profile of v1, /device:TPU:0, one launch (start us, length us, event | category | flops | bytes accessed | tf_op | source)
XLA Modules:
  0.0 322.3 jit_solution(2565437563368995101)
XLA Ops:
  2.0 7.9 %all-to-all-start = ((bf16[8,8,512]{2,1,0:T(8,128)(2,1)}), bf16[8,8,512]{2,1,0:T(8,128)(2,1)S(1)}, u32[]{:S(2)}, u32[]{:S(2)}) async-start(bf16[8,8,512]{2,1,0:T(8,128)(2,1)} %broadcast_in_dim.46), calls=%async_computation | async-start | bytes 131072 | tf_op jit(solution)/shard_map/all_to_all | solution.py:854
  11.5 1.8 first_norm.1.p0
  13.3 4.3 %all-to-all-done = bf16[8,8,512]{2,1,0:T(8,128)(2,1)S(1)} async-done(((bf16[8,8,512]{2,1,0:T(8,128)(2,1)}), bf16[8,8,512]{2,1,0:T(8,128)(2,1)S(1)}, u32[]{:S(2)}, u32[]{:S(2)}) %all-to-all-start) | async-done | bytes 65568 | tf_op jit(solution)/shard_map/all_to_all | solution.py:854
  19.9 4.9 %all-to-all-start.1 = ((bf16[8,64,1152]{2,1,0:T(8,128)(2,1)}), bf16[8,64,1152]{2,1,0:T(8,128)(2,1)S(1)}, u32[]{:S(2)}, u32[]{:S(2)}) async-start(bf16[8,64,1152]{2,1,0:T(8,128)(2,1)} %broadcast_in_dim.47), calls=%async_computation.1 | async-start | bytes 2359296 | tf_op jit(solution)/shard_map/all_to_all | solution.py:854
  24.8 2.1 collective-permute-start.6
  26.9 2.1 collective-permute-start.5
  29.0 1.7 collective-permute-start.4
  30.7 3.4 %collective-permute-start.3 = (bf16[128,1024]{1,0:T(8,128)(2,1)S(1)}, bf16[128,1024]{1,0:T(8,128)(2,1)}, u32[]{:S(2)}, u32[]{:S(2)}) collective-permute-start(bf16[128,1024]{1,0:T(8,128)(2,1)S(1)} %copy-done.20), channel_id=1, source_target_pairs={{0,4},{1,5},{2,6},{3,7},{4,0},{5,1},{6,2},{7,3},{8,12},{9,13},{10,... | collective-permute-start | bytes 786440 | tf_op jit(solution)/shard_map/ppermute | solution.py:833
  34.1 14.3 %all-to-all-done.1.own_hbm = bf16[8,64,1152]{2,1,0:T(8,128)(2,1)S(1)} async-done(((bf16[8,64,1152]{2,1,0:T(8,128)(2,1)}), bf16[8,64,1152]{2,1,0:T(8,128)(2,1)S(1)}, u32[]{:S(2)}, u32[]{:S(2)}) %all-to-all-start.1) | async-done | bytes 1179680 | tf_op jit(solution)/shard_map/all_to_all | solution.py:854
  49.1 4.1 %collective-permute-done.6.p7 = bf16[128,1024]{1,0:T(8,128)(2,1)S(1)} collective-permute-done((bf16[128,1024]{1,0:T(8,128)(2,1)S(1)}, bf16[128,1024]{1,0:T(8,128)(2,1)S(1)}, u32[]{:S(2)}, u32[]{:S(2)}) %collective-permute-start.6) | collective-permute-done | bytes 262176 | tf_op jit(solution)/shard_map/ppermute | solution.py:833
  53.2 1.9 collective-permute-done.5.p6
  56.3 1.9 collective-permute-start
  63.5 6.9 %all-to-all-start.2 = ((bf16[16,64,768]{2,1,0:T(8,128)(2,1)}), bf16[16,64,768]{2,1,0:T(8,128)(2,1)S(1)}, u32[]{:S(2)}, u32[]{:S(2)}) async-start(bf16[16,64,768]{2,1,0:T(8,128)(2,1)} %broadcast_in_dim.48), calls=%async_computation.2 | async-start | bytes 3145728 | tf_op jit(solution)/shard_map/all_to_all | solution.py:854
  70.4 15.1 %mixer_forward.1 = (bf16[8,128,1024]{2,1,0:T(8,128)(2,1)}, bf16[1024,1024]{1,0:T(8,128)(2,1)}, f32[1024,1024]{1,0:T(8,128)}, f32[1024,256]{1,0:T(8,128)}, bf16[1...) custom-call(s32[3]{0:T(128)} %pad_add_fusion.core_ref, bf16[128,1024]{1,0:T(8,128)(2,1)} %first_norm.1.p0, ...), custom_call_target="tpu_custom_call" | custom-call | flops 20000000000 | bytes 40000000 | tf_op jit(solution)/shard_map/mixer_forward/pallas_call | solution.py:717
  85.5 6.5 %all-to-all-done.2 = bf16[16,64,768]{2,1,0:T(8,128)(2,1)S(1)} async-done(((bf16[16,64,768]{2,1,0:T(8,128)(2,1)}), bf16[16,64,768]{2,1,0:T(8,128)(2,1)S(1)}, u32[]{:S(2)}, u32[]{:S(2)}) %all-to-all-start.2) | async-done | bytes 1572896 | tf_op jit(solution)/shard_map/all_to_all | solution.py:854
  93.2 4.7 %all-to-all-start.3 = ((bf16[8,128,1024]{2,1,0:T(8,128)(2,1)}), bf16[8,128,1024]{2,1,0:T(8,128)(2,1)S(1)}, u32[]{:S(2)}, u32[]{:S(2)}) async-start(bf16[8,128,1024]{2,1,0:T(8,128)(2,1)} %bitcast.64), calls=%async_computation.3 | async-start | bytes 4194304 | tf_op jit(solution)/shard_map/all_to_all | solution.py:854
  97.9 4.5 %collective-permute-start.10 = (bf16[128,1024]{1,0:T(8,128)(2,1)S(1)}, bf16[128,1024]{1,0:T(8,128)(2,1)S(1)}, u32[]{:S(2)}, u32[]{:S(2)}) collective-permute-start(bf16[128,1024]{1,0:T(8,128)(2,1)S(1)} %bitcast.60), channel_id=1, source_target_pairs={{0,3},{1,2},{2,1},{3,0},{4,7},{5,6},{6,5},{7,4},{8,11},{9,10},{10,... | collective-permute-start | bytes 786440 | tf_op jit(solution)/shard_map/ppermute | solution.py:833
  103.1 29.5 %collective-permute-done.10.c3 = bf16[128,1024]{1,0:T(8,128)(2,1)S(1)} collective-permute-done((bf16[128,1024]{1,0:T(8,128)(2,1)S(1)}, bf16[128,1024]{1,0:T(8,128)(2,1)S(1)}, u32[]{:S(2)}, u32[]{:S(2)}) %collective-permute-start.10) | collective-permute-done | bytes 262176 | tf_op jit(solution)/shard_map/ppermute | solution.py:833
  134.1 2.9 second_norm.1
  137.0 3.1 collective-permute-start.13
  140.0 1.7 collective-permute-start.12
  141.9 4.8 %collective-permute-done.13.n3 = bf16[128,1024]{1,0:T(8,128)(2,1)S(1)} collective-permute-done((bf16[128,1024]{1,0:T(8,128)(2,1)}, bf16[128,1024]{1,0:T(8,128)(2,1)S(1)}, u32[]{:S(2)}, u32[]{:S(2)}) %collective-permute-start.13) | collective-permute-done | bytes 262176 | tf_op jit(solution)/shard_map/ppermute | solution.py:833
  146.8 2.4 collective-permute-done.12.n2
  150.6 8.3 %feed.1 = (bf16[128,1024]{1,0:T(8,128)(2,1)}, bf16[128,1024]{1,0:T(8,128)(2,1)}, bf16[128,1024]{1,0:T(8,128)(2,1)}, bf16[128,1024]{1,0:T(8,128)(2,1)}, bf16[128,...) custom-call(s32[3]{0:T(128)} %pad_add_fusion.core_ref, ...), custom_call_target="tpu_custom_call" | custom-call | flops 50000000 | bytes 100000 | tf_op jit(solution)/shard_map/feed/pallas_call | solution.py:717
  158.9 2.3 collective-permute-start.15
  161.2 2.1 collective-permute-start.16
  164.1 5.5 %feed_weights.1 = (bf16[2,8,64,768]{3,2,1,0:T(8,128)(2,1)}, bf16[2,8,64,768]{3,2,1,0:T(8,128)(2,1)}) custom-call(s32[3]{0:T(128)} %pad_add_fusion.core_ref, bf16[128,1024]{1,0:T(8,128)(2,1)} %get-tuple-element.109.n0, bf16[128,1024]{1,0:T(8,128)(2,1)} %copy-done.13, bf16[128,1024]{1,0:T(8,128)(2,1)} %copy-done.12, bf16[128,1024]{1,0:T(8,128)(2,1)} %copy-done.11, ...), custom_call_target="tpu_custom_call" | custom-call | flops 50000000 | bytes 100000 | tf_op jit(solution)/shard_map/feed_weights/pallas_call | solution.py:717
  170.8 3.5 %collective-permute-done.17.s3 = bf16[128,1024]{1,0:T(8,128)(2,1)S(1)} collective-permute-done((bf16[128,1024]{1,0:T(8,128)(2,1)}, bf16[128,1024]{1,0:T(8,128)(2,1)S(1)}, u32[]{:S(2)}, u32[]{:S(2)}) %collective-permute-start.17) | collective-permute-done | bytes 262176 | tf_op jit(solution)/shard_map/ppermute | solution.py:833
  175.0 3.4 %hidden_grad.1 = (f32[128,1024]{1,0:T(8,128)}, bf16[8,128,1024]{2,1,0:T(8,128)(2,1)}) custom-call(f32[128,1024]{1,0:T(8,128)} %get-tuple-element.124.hidden_ref, f32[1,1024]{1,0:T(1,128)} %bitcast.76, bf16[128,1024]{1,0:T(8,128)(2,1)} %bitcast.59, bf16[128,1024]{1,0:T(8,128)(2,1)} %get-tuple-element.125.s0, bf16[128,1024]{1,0:T(8,128)(2,1)} %copy-done.17, ...), custom_call_target="tpu_custom_call" | custom-call | flops 50000000 | bytes 100000 | tf_op jit(solution)/shard_map/hidden_grad/pallas_call | solution.py:717
  178.4 7.1 %all-to-all-start.4 = ((bf16[8,128,1024]{2,1,0:T(8,128)(2,1)}), bf16[8,128,1024]{2,1,0:T(8,128)(2,1)S(1)}, u32[]{:S(2)}, u32[]{:S(2)}) async-start(bf16[8,128,1024]{2,1,0:T(8,128)(2,1)} %get-tuple-element.129), calls=%async_computation.4 | async-start | bytes 4194304 | tf_op jit(solution)/shard_map/all_to_all | solution.py:854
  185.5 3.5 %collective-permute-start.21 = (bf16[128,1024]{1,0:T(8,128)(2,1)}, bf16[128,1024]{1,0:T(8,128)(2,1)S(1)}, u32[]{:S(2)}, u32[]{:S(2)}) collective-permute-start(bf16[128,1024]{1,0:T(8,128)(2,1)} %get-tuple-element.143), channel_id=1, source_target_pairs={{0,1},{1,0},{2,3},{3,2},{4,5},{5,4},{6,7},{7,6},{8,9},{9,8},{10,11... | collective-permute-start | bytes 786440 | tf_op jit(solution)/shard_map/ppermute | solution.py:833
  190.6 3.4 %feed_pair.1 = bf16[2,8,64,768]{3,2,1,0:T(8,128)(2,1)} custom-call(bf16[2,8,64,768]{3,2,1,0:T(8,128)(2,1)} %get-tuple-element.122.keep_ref, bf16[2,8,64,768]{3,2,1,0:T(8,128)(2,1)} %collective-permute-done.18.come_ref), custom_call_target="tpu_custom_call" | custom-call | flops 50000000 | bytes 100000 | tf_op jit(solution)/shard_map/feed_pair/pallas_call | solution.py:717
  194.0 21.1 %all-to-all-done.4 = bf16[8,128,1024]{2,1,0:T(8,128)(2,1)S(1)} async-done(((bf16[8,128,1024]{2,1,0:T(8,128)(2,1)}), bf16[8,128,1024]{2,1,0:T(8,128)(2,1)S(1)}, u32[]{:S(2)}, u32[]{:S(2)}) %all-to-all-start.4) | async-done | bytes 2097184 | tf_op jit(solution)/shard_map/all_to_all | solution.py:854
  216.4 6.5 %all-to-all-start.5 = ((bf16[16,64,768]{2,1,0:T(8,128)(2,1)}), bf16[16,64,768]{2,1,0:T(8,128)(2,1)}, u32[]{:S(2)}, u32[]{:S(2)}) async-start(bf16[16,64,768]{2,1,0:T(8,128)(2,1)} %bitcast.53), calls=%async_computation.5 | async-start | bytes 3145728 | tf_op jit(solution)/shard_map/all_to_all | solution.py:854
  222.9 26.6 %mixer_backward.1 = (bf16[1024,1024]{1,0:T(8,128)(2,1)}, bf16[1024,896]{1,0:T(8,128)(2,1)}, f32[16,384]{1,0:T(8,128)}) custom-call(s32[3]{0:T(128)} %pad_add_fusion.core_ref, bf16[1024,1024]{1,0:T(8,128)(2,1)} %bitcast.49, bf16[8,64,1152]{2,1,0:T(8,128)(2,1)} %copy-done.6, bf16[8,64,1152]{2,1,0:T(8,128)(2,1)} %collective-permute-done.7.mate_hbm, ...), custom_call_target="tpu_custom_call" | custom-call | flops 32999999488 | bytes 66000000 | tf_op jit(solution)/shard_map/mixer_backward/pallas_call | solution.py:717
  250.4 6.0 %all-to-all-start.6 = ((bf16[8,128,1024]{2,1,0:T(8,128)(2,1)}), bf16[8,128,1024]{2,1,0:T(8,128)(2,1)S(1)}, u32[]{:S(2)}, u32[]{:S(2)}) async-start(bf16[8,128,1024]{2,1,0:T(8,128)(2,1)} %bitcast.63), calls=%async_computation.6 | async-start | bytes 4194304 | tf_op jit(solution)/shard_map/all_to_all | solution.py:854
  256.3 7.2 %mixer_weights.1 = (bf16[8,64,1152]{2,1,0:T(8,128)(2,1)}, bf16[8,64,1152]{2,1,0:T(8,128)(2,1)}) custom-call(s32[3]{0:T(128)} %pad_add_fusion.core_ref, bf16[8,128,1024]{2,1,0:T(8,128)(2,1)} %get-tuple-element.102.normed_hbm.normed_ref, bf16[1024,896]{1,0:T(8,128)(2,1)} %get-tuple-element.136.dproj_ref, bf16[1024,1024]{1,0:T(8,128)(2,1)} %bitcast.50, ...), custom_call_target="tpu_custom_call" | custom-call | flops 50000000 | bytes 100000 | tf_op jit(solution)/shard_map/mixer_weights/pallas_call | solution.py:717
  264.2 2.0 collective-permute-done.20.small_come_ref
  267.7 3.0 mixer_pair.1
  270.8 10.0 %all-to-all-done.6.blocks_ref = bf16[8,128,1024]{2,1,0:T(8,128)(2,1)S(1)} async-done(((bf16[8,128,1024]{2,1,0:T(8,128)(2,1)}), bf16[8,128,1024]{2,1,0:T(8,128)(2,1)S(1)}, u32[]{:S(2)}, u32[]{:S(2)}) %all-to-all-start.6) | async-done | bytes 2097184 | tf_op jit(solution)/shard_map/all_to_all | solution.py:854
  280.8 4.6 %all-to-all-start.7 = ((bf16[8,80,1152]{2,1,0:T(8,128)(2,1)}), bf16[8,80,1152]{2,1,0:T(8,128)(2,1)}, u32[]{:S(2)}, u32[]{:S(2)}) async-start(bf16[8,80,1152]{2,1,0:T(8,128)(2,1)} %mixer_pair.1), calls=%async_computation.7 | async-start | bytes 2949120 | tf_op jit(solution)/shard_map/all_to_all | solution.py:854
  285.4 2.2 output.1
  287.6 1.6 convert_reduce_fusion
  289.9 3.1 input_grad.1
  293.0 9.8 %all-to-all-done.7.blocks_ref = bf16[8,80,1152]{2,1,0:T(8,128)(2,1)} async-done(((bf16[8,80,1152]{2,1,0:T(8,128)(2,1)}), bf16[8,80,1152]{2,1,0:T(8,128)(2,1)}, u32[]{:S(2)}, u32[]{:S(2)}) %all-to-all-start.7) | async-done | bytes 1474592 | tf_op jit(solution)/shard_map/all_to_all | solution.py:854
  302.8 2.4 collect.1
  305.1 5.3 %all-to-all-start.8 = ((f32[8,24,512]{2,1,0:T(8,128)}), f32[8,24,512]{2,1,0:T(8,128)S(1)}, u32[]{:S(2)}, u32[]{:S(2)}) async-start(f32[8,24,512]{2,1,0:T(8,128)} %get-tuple-element.158), calls=%async_computation.8 | async-start | bytes 786432 | tf_op jit(solution)/shard_map/all_to_all | solution.py:854
  317.5 2.4 all-to-all-done.8.lines_ref
  (151 shorter events, 35.7 us)
Async XLA Ops:
  2.0 15.6 %all-to-all-start = ((bf16[8,8,512]{2,1,0:T(8,128)(2,1)}), bf16[8,8,512]{2,1,0:T(8,128)(2,1)S(1)}, u32[]{:S(2)}, u32[]{:S(2)}) async-start(bf16[8,8,512]{2,1,0:T(8,128)(2,1)} %broadcast_in_dim.46), calls=%async_computation | async-start | bytes 131072 | tf_op jit(solution)/shard_map/all_to_all | solution.py:854
  18.7 29.7 %copy-start.26 = (s32[1,1024]{1,0:T(1,128)S(1)}, s32[1,1024]{1,0:T(1,128)}, u32[]{:S(2)}) copy-start(s32[1,1024]{1,0:T(1,128)} %param.23) | copy-start | bytes 12292
  19.8 38.3 %copy-start.27 = (f32[4,192]{1,0:T(4,128)S(1)}, f32[4,192]{1,0:T(4,128)}, u32[]{:S(2)}) copy-start(f32[4,192]{1,0:T(4,128)} %param.29) | copy-start | bytes 9220
  19.8 38.3 %copy-start.28 = (f32[4,256]{1,0:T(4,128)S(1)}, f32[4,256]{1,0:T(4,128)}, u32[]{:S(2)}) copy-start(f32[4,256]{1,0:T(4,128)} %param.30) | copy-start | bytes 12292
  19.8 38.4 %copy-start.30 = (f32[3]{0:T(128)S(1)}, f32[3]{0:T(128)}, u32[]{:S(2)}) copy-start(f32[3]{0:T(128)} %param.31) | copy-start | bytes 40
  19.8 38.4 %copy-start.31 = (f32[3]{0:T(128)S(1)}, f32[3]{0:T(128)}, u32[]{:S(2)}) copy-start(f32[3]{0:T(128)} %param.32) | copy-start | bytes 40
  19.9 38.5 %copy-start.29 = (f32[3]{0:T(128)S(1)}, f32[3]{0:T(128)}, u32[]{:S(2)}) copy-start(f32[3]{0:T(128)} %param.33) | copy-start | bytes 40
  19.9 28.5 %all-to-all-start.1 = ((bf16[8,64,1152]{2,1,0:T(8,128)(2,1)}), bf16[8,64,1152]{2,1,0:T(8,128)(2,1)S(1)}, u32[]{:S(2)}, u32[]{:S(2)}) async-start(bf16[8,64,1152]{2,1,0:T(8,128)(2,1)} %broadcast_in_dim.47), calls=%async_computation.1 | async-start | bytes 2359296 | tf_op jit(solution)/shard_map/all_to_all | solution.py:854
  24.8 36.7 %copy-start.21 = (bf16[256,64]{0,1:T(8,128)(2,1)S(1)}, bf16[256,64]{0,1:T(8,128)(2,1)}, u32[]{:S(2)}) copy-start(bf16[256,64]{0,1:T(8,128)(2,1)} %param.41) | copy-start | bytes 98308
  24.8 36.7 %copy-start.22 = (bf16[64,256]{1,0:T(8,128)(2,1)S(1)}, bf16[64,256]{1,0:T(8,128)(2,1)}, u32[]{:S(2)}) copy-start(bf16[64,256]{1,0:T(8,128)(2,1)} %param.40) | copy-start | bytes 98308
  24.8 36.7 %copy-start.23 = (bf16[64,256]{1,0:T(8,128)(2,1)S(1)}, bf16[64,256]{1,0:T(8,128)(2,1)}, u32[]{:S(2)}) copy-start(bf16[64,256]{1,0:T(8,128)(2,1)} %param.39) | copy-start | bytes 98308
  24.8 28.4 %collective-permute-start.6 = (bf16[128,1024]{1,0:T(8,128)(2,1)S(1)}, bf16[128,1024]{1,0:T(8,128)(2,1)S(1)}, u32[]{:S(2)}, u32[]{:S(2)}) collective-permute-start(bf16[128,1024]{1,0:T(8,128)(2,1)S(1)} %copy-done.20), channel_id=1, source_target_pairs={{0,7},{1,6},{2,5},{3,4},{4,3},{5,2},{6,1},{7,0},{8,15},{9,14},{10,... | collective-permute-start | bytes 786440 | tf_op jit(solution)/shard_map/ppermute | solution.py:833
  26.9 28.1 %collective-permute-start.5 = (bf16[128,1024]{1,0:T(8,128)(2,1)S(1)}, bf16[128,1024]{1,0:T(8,128)(2,1)S(1)}, u32[]{:S(2)}, u32[]{:S(2)}) collective-permute-start(bf16[128,1024]{1,0:T(8,128)(2,1)S(1)} %copy-done.20), channel_id=1, source_target_pairs={{0,6},{1,7},{2,4},{3,5},{4,2},{5,3},{6,0},{7,1},{8,14},{9,15},{10,... | collective-permute-start | bytes 786440 | tf_op jit(solution)/shard_map/ppermute | solution.py:833
  29.0 27.3 %collective-permute-start.4 = (bf16[128,1024]{1,0:T(8,128)(2,1)S(1)}, bf16[128,1024]{1,0:T(8,128)(2,1)S(1)}, u32[]{:S(2)}, u32[]{:S(2)}) collective-permute-start(bf16[128,1024]{1,0:T(8,128)(2,1)S(1)} %copy-done.20), channel_id=1, source_target_pairs={{0,5},{1,4},{2,7},{3,6},{4,1},{5,0},{6,3},{7,2},{8,13},{9,12},{10,... | collective-permute-start | bytes 786440 | tf_op jit(solution)/shard_map/ppermute | solution.py:833
  30.7 39.7 %collective-permute-start.3 = (bf16[128,1024]{1,0:T(8,128)(2,1)S(1)}, bf16[128,1024]{1,0:T(8,128)(2,1)}, u32[]{:S(2)}, u32[]{:S(2)}) collective-permute-start(bf16[128,1024]{1,0:T(8,128)(2,1)S(1)} %copy-done.20), channel_id=1, source_target_pairs={{0,4},{1,5},{2,6},{3,7},{4,0},{5,1},{6,2},{7,3},{8,12},{9,13},{10,... | collective-permute-start | bytes 786440 | tf_op jit(solution)/shard_map/ppermute | solution.py:833
  48.4 15.1 %copy-start.6 = (bf16[8,64,1152]{2,1,0:T(8,128)(2,1)}, bf16[8,64,1152]{2,1,0:T(8,128)(2,1)S(1)}, u32[]{:S(2)}) copy-start(bf16[8,64,1152]{2,1,0:T(8,128)(2,1)S(1)} %all-to-all-done.1.own_hbm) | copy-start | bytes 3538948
  48.4 22.1 %collective-permute-start.7 = (bf16[8,64,1152]{2,1,0:T(8,128)(2,1)S(1)}, bf16[8,64,1152]{2,1,0:T(8,128)(2,1)}, u32[]{:S(2)}, u32[]{:S(2)}) collective-permute-start(bf16[8,64,1152]{2,1,0:T(8,128)(2,1)S(1)} %all-to-all-done.1.own_hbm), channel_id=1, source_target_pairs={{0,8},{8,0},{1,9},{9,1},{2,10},{10,2},{3,11},{11,3},{4,12},{12,4},... | collective-permute-start | bytes 3538952 | tf_op jit(solution)/shard_map/ppermute | solution.py:833
  53.2 17.2 %collective-permute-start.2 = (bf16[128,1024]{1,0:T(8,128)(2,1)S(1)}, bf16[128,1024]{1,0:T(8,128)(2,1)}, u32[]{:S(2)}, u32[]{:S(2)}) collective-permute-start(bf16[128,1024]{1,0:T(8,128)(2,1)S(1)} %copy-done.20), channel_id=1, source_target_pairs={{0,3},{1,2},{2,1},{3,0},{4,7},{5,6},{6,5},{7,4},{8,11},{9,10},{10,... | collective-permute-start | bytes 786440 | tf_op jit(solution)/shard_map/ppermute | solution.py:833
  55.1 15.4 %collective-permute-start.1 = (bf16[128,1024]{1,0:T(8,128)(2,1)S(1)}, bf16[128,1024]{1,0:T(8,128)(2,1)}, u32[]{:S(2)}, u32[]{:S(2)}) collective-permute-start(bf16[128,1024]{1,0:T(8,128)(2,1)S(1)} %copy-done.20), channel_id=1, source_target_pairs={{0,2},{1,3},{2,0},{3,1},{4,6},{5,7},{6,4},{7,5},{8,10},{9,11},{10,... | collective-permute-start | bytes 786440 | tf_op jit(solution)/shard_map/ppermute | solution.py:833
  56.3 14.1 %collective-permute-start = (bf16[128,1024]{1,0:T(8,128)(2,1)S(1)}, bf16[128,1024]{1,0:T(8,128)(2,1)}, u32[]{:S(2)}, u32[]{:S(2)}) collective-permute-start(bf16[128,1024]{1,0:T(8,128)(2,1)S(1)} %copy-done.20), channel_id=1, source_target_pairs={{0,1},{1,0},{2,3},{3,2},{4,5},{5,4},{6,7},{7,6},{8,9},{9,8},{10,11... | collective-permute-start | bytes 786440 | tf_op jit(solution)/shard_map/ppermute | solution.py:833
  63.5 28.6 %all-to-all-start.2 = ((bf16[16,64,768]{2,1,0:T(8,128)(2,1)}), bf16[16,64,768]{2,1,0:T(8,128)(2,1)S(1)}, u32[]{:S(2)}, u32[]{:S(2)}) async-start(bf16[16,64,768]{2,1,0:T(8,128)(2,1)} %broadcast_in_dim.48), calls=%async_computation.2 | async-start | bytes 3145728 | tf_op jit(solution)/shard_map/all_to_all | solution.py:854
  93.2 39.4 %all-to-all-start.3 = ((bf16[8,128,1024]{2,1,0:T(8,128)(2,1)}), bf16[8,128,1024]{2,1,0:T(8,128)(2,1)S(1)}, u32[]{:S(2)}, u32[]{:S(2)}) async-start(bf16[8,128,1024]{2,1,0:T(8,128)(2,1)} %bitcast.64), calls=%async_computation.3 | async-start | bytes 4194304 | tf_op jit(solution)/shard_map/all_to_all | solution.py:854
  97.9 44.1 %collective-permute-start.14 = (bf16[2,8,64,768]{3,2,1,0:T(8,128)(2,1)}, bf16[2,8,64,768]{3,2,1,0:T(8,128)(2,1)}, u32[]{:S(2)}, u32[]{:S(2)}) collective-permute-start(bf16[2,8,64,768]{3,2,1,0:T(8,128)(2,1)} %bitcast.51), channel_id=1, source_target_pairs={{0,8},{8,0},{1,9},{9,1},{2,10},{10,2},{3,11},{11,3},{4,12},{12,4},... | collective-permute-start | bytes 4718600 | tf_op jit(solution)/shard_map/ppermute | solution.py:833
  97.9 34.7 %collective-permute-start.10 = (bf16[128,1024]{1,0:T(8,128)(2,1)S(1)}, bf16[128,1024]{1,0:T(8,128)(2,1)S(1)}, u32[]{:S(2)}, u32[]{:S(2)}) collective-permute-start(bf16[128,1024]{1,0:T(8,128)(2,1)S(1)} %bitcast.60), channel_id=1, source_target_pairs={{0,3},{1,2},{2,1},{3,0},{4,7},{5,6},{6,5},{7,4},{8,11},{9,10},{10,... | collective-permute-start | bytes 786440 | tf_op jit(solution)/shard_map/ppermute | solution.py:833
  102.4 30.2 %collective-permute-start.9 = (bf16[128,1024]{1,0:T(8,128)(2,1)S(1)}, bf16[128,1024]{1,0:T(8,128)(2,1)S(1)}, u32[]{:S(2)}, u32[]{:S(2)}) collective-permute-start(bf16[128,1024]{1,0:T(8,128)(2,1)S(1)} %bitcast.61), channel_id=1, source_target_pairs={{0,2},{1,3},{2,0},{3,1},{4,6},{5,7},{6,4},{7,5},{8,10},{9,11},{10,... | collective-permute-start | bytes 786440 | tf_op jit(solution)/shard_map/ppermute | solution.py:833
  103.0 29.6 %collective-permute-start.8 = (bf16[128,1024]{1,0:T(8,128)(2,1)S(1)}, bf16[128,1024]{1,0:T(8,128)(2,1)S(1)}, u32[]{:S(2)}, u32[]{:S(2)}) collective-permute-start(bf16[128,1024]{1,0:T(8,128)(2,1)S(1)} %bitcast.62), channel_id=1, source_target_pairs={{0,1},{1,0},{2,3},{3,2},{4,5},{5,4},{6,7},{7,6},{8,9},{9,8},{10,11... | collective-permute-start | bytes 786440 | tf_op jit(solution)/shard_map/ppermute | solution.py:833
  132.6 17.3 %copy-start.8 = (bf16[128,1024]{1,0:T(8,128)(2,1)}, bf16[128,1024]{1,0:T(8,128)(2,1)S(1)}, u32[]{:S(2)}) copy-start(bf16[128,1024]{1,0:T(8,128)(2,1)S(1)} %collective-permute-done.10.c3) | copy-start | bytes 786436
  132.6 17.3 %copy-start.9 = (bf16[128,1024]{1,0:T(8,128)(2,1)}, bf16[128,1024]{1,0:T(8,128)(2,1)S(1)}, u32[]{:S(2)}) copy-start(bf16[128,1024]{1,0:T(8,128)(2,1)S(1)} %collective-permute-done.9.c2) | copy-start | bytes 786436
  132.6 17.3 %copy-start.10 = (bf16[128,1024]{1,0:T(8,128)(2,1)}, bf16[128,1024]{1,0:T(8,128)(2,1)S(1)}, u32[]{:S(2)}) copy-start(bf16[128,1024]{1,0:T(8,128)(2,1)S(1)} %collective-permute-done.8.c1) | copy-start | bytes 786436
  137.0 9.8 %collective-permute-start.13 = (bf16[128,1024]{1,0:T(8,128)(2,1)}, bf16[128,1024]{1,0:T(8,128)(2,1)S(1)}, u32[]{:S(2)}, u32[]{:S(2)}) collective-permute-start(bf16[128,1024]{1,0:T(8,128)(2,1)} %get-tuple-element.109.n0), channel_id=1, source_target_pairs={{0,3},{1,2},{2,1},{3,0},{4,7},{5,6},{6,5},{7,4},{8,11},{9,10},{10,... | collective-permute-start | bytes 786440 | tf_op jit(solution)/shard_map/ppermute | solution.py:833
  140.0 9.2 %collective-permute-start.12 = (bf16[128,1024]{1,0:T(8,128)(2,1)}, bf16[128,1024]{1,0:T(8,128)(2,1)S(1)}, u32[]{:S(2)}, u32[]{:S(2)}) collective-permute-start(bf16[128,1024]{1,0:T(8,128)(2,1)} %get-tuple-element.109.n0), channel_id=1, source_target_pairs={{0,2},{1,3},{2,0},{3,1},{4,6},{5,7},{6,4},{7,5},{8,10},{9,11},{10,... | collective-permute-start | bytes 786440 | tf_op jit(solution)/shard_map/ppermute | solution.py:833
  141.8 8.1 %collective-permute-start.11 = (bf16[128,1024]{1,0:T(8,128)(2,1)}, bf16[128,1024]{1,0:T(8,128)(2,1)S(1)}, u32[]{:S(2)}, u32[]{:S(2)}) collective-permute-start(bf16[128,1024]{1,0:T(8,128)(2,1)} %get-tuple-element.109.n0), channel_id=1, source_target_pairs={{0,1},{1,0},{2,3},{3,2},{4,5},{5,4},{6,7},{7,6},{8,9},{9,8},{10,11... | collective-permute-start | bytes 786440 | tf_op jit(solution)/shard_map/ppermute | solution.py:833
  158.9 10.8 %collective-permute-start.15 = (bf16[128,1024]{1,0:T(8,128)(2,1)}, bf16[128,1024]{1,0:T(8,128)(2,1)S(1)}, u32[]{:S(2)}, u32[]{:S(2)}) collective-permute-start(bf16[128,1024]{1,0:T(8,128)(2,1)} %get-tuple-element.119), channel_id=1, source_target_pairs={{0,1},{1,0},{2,3},{3,2},{4,5},{5,4},{6,7},{7,6},{8,9},{9,8},{10,11... | collective-permute-start | bytes 786440 | tf_op jit(solution)/shard_map/ppermute | solution.py:833
  161.2 9.5 %collective-permute-start.16 = (bf16[128,1024]{1,0:T(8,128)(2,1)}, bf16[128,1024]{1,0:T(8,128)(2,1)S(1)}, u32[]{:S(2)}, u32[]{:S(2)}) collective-permute-start(bf16[128,1024]{1,0:T(8,128)(2,1)} %get-tuple-element.120), channel_id=1, source_target_pairs={{0,2},{1,3},{2,0},{3,1},{4,6},{5,7},{6,4},{7,5},{8,10},{9,11},{10,... | collective-permute-start | bytes 786440 | tf_op jit(solution)/shard_map/ppermute | solution.py:833
  163.4 10.9 %collective-permute-start.17 = (bf16[128,1024]{1,0:T(8,128)(2,1)}, bf16[128,1024]{1,0:T(8,128)(2,1)S(1)}, u32[]{:S(2)}, u32[]{:S(2)}) collective-permute-start(bf16[128,1024]{1,0:T(8,128)(2,1)} %get-tuple-element.121), channel_id=1, source_target_pairs={{0,3},{1,2},{2,1},{3,0},{4,7},{5,6},{6,5},{7,4},{8,11},{9,10},{10,... | collective-permute-start | bytes 786440 | tf_op jit(solution)/shard_map/ppermute | solution.py:833
  178.4 10.6 %copy-start.36 = (bf16[128,1024]{1,0:T(8,128)(2,1)S(1)}, bf16[128,1024]{1,0:T(8,128)(2,1)}, u32[]{:S(2)}) copy-start(bf16[128,1024]{1,0:T(8,128)(2,1)} %get-tuple-element.144) | copy-start | bytes 786436
  178.4 12.1 %copy-start.35 = (bf16[128,1024]{1,0:T(8,128)(2,1)S(1)}, bf16[128,1024]{1,0:T(8,128)(2,1)}, u32[]{:S(2)}) copy-start(bf16[128,1024]{1,0:T(8,128)(2,1)} %get-tuple-element.145) | copy-start | bytes 786436
  178.4 36.7 %all-to-all-start.4 = ((bf16[8,128,1024]{2,1,0:T(8,128)(2,1)}), bf16[8,128,1024]{2,1,0:T(8,128)(2,1)S(1)}, u32[]{:S(2)}, u32[]{:S(2)}) async-start(bf16[8,128,1024]{2,1,0:T(8,128)(2,1)} %get-tuple-element.129), calls=%async_computation.4 | async-start | bytes 4194304 | tf_op jit(solution)/shard_map/all_to_all | solution.py:854
  185.5 5.1 %collective-permute-start.18 = (bf16[2,8,64,768]{3,2,1,0:T(8,128)(2,1)}, bf16[2,8,64,768]{3,2,1,0:T(8,128)(2,1)}, u32[]{:S(2)}, u32[]{:S(2)}) collective-permute-start(bf16[2,8,64,768]{3,2,1,0:T(8,128)(2,1)} %get-tuple-element.123), channel_id=1, source_target_pairs={{0,8},{8,0},{1,9},{9,1},{2,10},{10,2},{3,11},{11,3},{4,12},{12,4},... | collective-permute-start | bytes 4718600 | tf_op jit(solution)/shard_map/ppermute | solution.py:833
  185.5 64.0 %collective-permute-start.21 = (bf16[128,1024]{1,0:T(8,128)(2,1)}, bf16[128,1024]{1,0:T(8,128)(2,1)S(1)}, u32[]{:S(2)}, u32[]{:S(2)}) collective-permute-start(bf16[128,1024]{1,0:T(8,128)(2,1)} %get-tuple-element.143), channel_id=1, source_target_pairs={{0,1},{1,0},{2,3},{3,2},{4,5},{5,4},{6,7},{7,6},{8,9},{9,8},{10,11... | collective-permute-start | bytes 786440 | tf_op jit(solution)/shard_map/ppermute | solution.py:833
  189.0 60.5 %collective-permute-start.22 = (bf16[128,1024]{1,0:T(8,128)(2,1)S(1)}, bf16[128,1024]{1,0:T(8,128)(2,1)S(1)}, u32[]{:S(2)}, u32[]{:S(2)}) collective-permute-start(bf16[128,1024]{1,0:T(8,128)(2,1)S(1)} %copy-done.36), channel_id=1, source_target_pairs={{0,2},{1,3},{2,0},{3,1},{4,6},{5,7},{6,4},{7,5},{8,10},{9,11},{10,... | collective-permute-start | bytes 786440 | tf_op jit(solution)/shard_map/ppermute | solution.py:833
  190.5 59.0 %collective-permute-start.23 = (bf16[128,1024]{1,0:T(8,128)(2,1)S(1)}, bf16[128,1024]{1,0:T(8,128)(2,1)S(1)}, u32[]{:S(2)}, u32[]{:S(2)}) collective-permute-start(bf16[128,1024]{1,0:T(8,128)(2,1)S(1)} %copy-done.35), channel_id=1, source_target_pairs={{0,3},{1,2},{2,1},{3,0},{4,7},{5,6},{6,5},{7,4},{8,11},{9,10},{10,... | collective-permute-start | bytes 786440 | tf_op jit(solution)/shard_map/ppermute | solution.py:833
  216.4 33.1 %all-to-all-start.5 = ((bf16[16,64,768]{2,1,0:T(8,128)(2,1)}), bf16[16,64,768]{2,1,0:T(8,128)(2,1)}, u32[]{:S(2)}, u32[]{:S(2)}) async-start(bf16[16,64,768]{2,1,0:T(8,128)(2,1)} %bitcast.53), calls=%async_computation.5 | async-start | bytes 3145728 | tf_op jit(solution)/shard_map/all_to_all | solution.py:854
  250.4 30.4 %all-to-all-start.6 = ((bf16[8,128,1024]{2,1,0:T(8,128)(2,1)}), bf16[8,128,1024]{2,1,0:T(8,128)(2,1)S(1)}, u32[]{:S(2)}, u32[]{:S(2)}) async-start(bf16[8,128,1024]{2,1,0:T(8,128)(2,1)} %bitcast.63), calls=%async_computation.6 | async-start | bytes 4194304 | tf_op jit(solution)/shard_map/all_to_all | solution.py:854
  263.6 3.2 collective-permute-start.19
  263.7 2.5 collective-permute-start.20
  280.8 22.0 %all-to-all-start.7 = ((bf16[8,80,1152]{2,1,0:T(8,128)(2,1)}), bf16[8,80,1152]{2,1,0:T(8,128)(2,1)}, u32[]{:S(2)}, u32[]{:S(2)}) async-start(bf16[8,80,1152]{2,1,0:T(8,128)(2,1)} %mixer_pair.1), calls=%async_computation.7 | async-start | bytes 2949120 | tf_op jit(solution)/shard_map/all_to_all | solution.py:854
  305.1 14.8 %all-to-all-start.8 = ((f32[8,24,512]{2,1,0:T(8,128)}), f32[8,24,512]{2,1,0:T(8,128)S(1)}, u32[]{:S(2)}, u32[]{:S(2)}) async-start(f32[8,24,512]{2,1,0:T(8,128)} %get-tuple-element.158), calls=%async_computation.8 | async-start | bytes 786432 | tf_op jit(solution)/shard_map/all_to_all | solution.py:854
  (22 other events, 64.0 us)
